TPU v7x, 32 devices: a whole 2x2x4 slice. The times are simulated.
32 devices in a mesh: groups: 2 (over x), src: 8 (over z, y), tgt: 2 (over core).
Axes of the slice: x: 2, y: 2, z: 4, core: 2. Of those that a mesh axis runs over, the one named last changes fastest.
Arguments:
- source_embed: bfloat16 [32768, 256], P(('groups', 'src')), parts along dimension 0, may hold values from -7 to 7
- target_embed: bfloat16 [32768, 256], P(('groups', 'tgt', 'src')), parts along dimension 0, may hold values from -6 to 6
- source_mass: float32 [32768], P(('groups', 'src')), parts along dimension 0, may hold values from 0.05 to 20
- target_mass: float32 [32768], P(('groups', 'tgt')), parts along dimension 0, may hold values from 0.05 to 20
- target_start: float32 [32768], P(('groups', 'tgt')), parts along dimension 0, may hold values from -3 to 11
- tile_list: int32 [16, 2, 2, 128], P(('groups', 'src'), 'tgt'), parts along dimension 0, may hold values from 0 to 63, as said below
- tile_count: int32 [16, 2], P(('groups', 'src'), 'tgt'), parts along dimension 0, may hold values from 25 to 128, as said below
Outputs:
- source_potential: float32 [32768], P(('groups', 'src')), parts along dimension 0
- target_potential: float32 [32768], P(('groups', 'tgt')), parts along dimension 0
There are 2 independent parts, one for each index of `groups`. A program takes and returns all parts, laid end to end along the dimension named above; each array names one. Nothing has to cross between parts.
Inputs may be any that keep to these rules, and one draw needn't show every extreme that they name: `tile_list`: entry [s, t, 0, k] is a row block among the 16 blocks of src index s, entry [s, t, 1, k] a column block among the 64 blocks of tgt index t. The 128 tiles of a device are distinct; its first 16 are (r, (r + s * 16) mod 64) for r = 0 .. 15, so every row and every column of the whole has support. `tile_count`: number of live tiles of a device, which are the first ones of its list; in every part one device holds 128.
All inputs are finite; a program needn't handle non-finite values.
Results may differ from a plain program's by a relative error of at most 0.0004.
Values may be sent and summed in bfloat16 or wider, within the bound.
No kernel may reach another device: no remote copies, remote signals or barrier semaphores. Data moves between devices by JAX's collectives and lax.ppermute only.
A program may use at most 64 MiB of HBM per device.

v0:
```python
import math

import jax
import jax.numpy as jnp
from jax import lax
from jax.experimental import pallas as pl
from jax.experimental.pallas import tpu as pltpu
from jax.sharding import PartitionSpec as P

TILE = 128
EPSILON = 0.05
FLOOR = -1e30
UNROLL = 4
CHUNKS = 2
VMEM_LIMIT = 48 * 1024 * 1024


def hop(value, src_mask, tgt_mask=0):
    cores = lax.axis_size("tgt")
    total = lax.axis_size("src") * cores
    flip = src_mask * cores + tgt_mask
    return lax.ppermute(value, ("src", "tgt"), [(i, i ^ flip) for i in range(total)])


def half_norms(rows):
    wide = rows.astype(jnp.float32)
    return 0.5 * jnp.sum(wide * wide, axis=-1).reshape(-1, TILE)


def list_kernel(src_rows, col_blocks, meta, own, peer, rows, cols, total):
    upper = meta[0]
    slots = own.shape[1]

    def clear(i, carry):
        rows[i] = 0
        cols[i] = 0
        return carry

    lax.fori_loop(0, rows.shape[0], clear, 0)

    def scan(refs, shift):
        def step(k, found):
            col = refs[1, k] - upper * col_blocks
            rows[found] = refs[0, k] + shift * src_rows
            cols[found] = col
            return found + ((col >= 0) & (col < col_blocks)).astype(jnp.int32)

        return step

    found = lax.fori_loop(0, jnp.minimum(own[2, 0], slots), scan(own, upper), 0)
    found = lax.fori_loop(0, jnp.minimum(peer[2, 0], slots), scan(peer, 1 - upper), found)
    rows[found] = 0
    cols[found] = 0
    total[0] = found


def merge_logs(parts, scale):
    peak = parts[0]
    for part in parts[1:]:
        peak = jnp.maximum(peak, part)
    summed = sum(jnp.exp2((part - peak) * scale) for part in parts)
    return peak + jnp.log2(summed) / scale


def pass_kernel(
    scale, by_row, first, places, has_out, meta, rows, cols, total, *refs
):
    n_parts, n_src, n_tgt = places
    parts, refs = refs[:n_parts], refs[n_parts:]
    aux, refs = refs[0], refs[1:]
    src_pieces, refs = refs[: len(n_src)], refs[len(n_src) :]
    tgt_pieces, refs = refs[: len(n_tgt)], refs[len(n_tgt) :]
    out, refs = refs[0], refs[1:]
    if has_out:
        extra, refs = refs[0], refs[1:]
    src, tgt, spread, peaks, sums, sems = refs
    copies = []
    for ref, place in zip(src_pieces, n_src):
        start = pl.multiple_of(place(meta), ref.shape[0])
        copies.append((ref, src.at[pl.ds(start, ref.shape[0])]))
    for ref, place in zip(tgt_pieces, n_tgt):
        start = pl.multiple_of(place(meta), ref.shape[0])
        copies.append((ref, tgt.at[pl.ds(start, ref.shape[0])]))
    moves = [pltpu.make_async_copy(a, b, sems.at[i]) for i, (a, b) in enumerate(copies)]
    for move in moves:
        move.start()
    peaks[...] = jnp.full(peaks.shape, FLOOR, jnp.float32)
    sums[...] = jnp.zeros(sums.shape, jnp.float32)
    if first:
        potential = parts[0][...]
    else:
        potential = aux[...] - merge_logs([part[...] for part in parts], scale)
    if has_out:
        extra[...] = potential
    turned = jnp.transpose(potential)
    for block in range(potential.shape[0]):
        spread[block] = jnp.broadcast_to(turned[:, block : block + 1], (TILE, TILE))
    for move in moves:
        move.wait()
    known, reduced = (tgt, src) if by_row else (src, tgt)
    known_ids, reduced_ids = (cols, rows) if by_row else (rows, cols)
    dummy = peaks.shape[0] - 1
    count = total[0]

    def merge(carry):
        for place, peak, summed in carry:
            old_peak = peaks[place]
            old_sum = sums[place]
            top = jnp.maximum(old_peak, peak)
            peaks[place] = top
            sums[place] = old_sum * jnp.exp2((old_peak - top) * scale) + summed * jnp.exp2(
                (peak - top) * scale
            )

    def turn(index, carry):
        merge(carry)
        found = []
        for lane in range(UNROLL):
            slot = index * UNROLL + lane
            known_id, reduced_id = known_ids[slot], reduced_ids[slot]
            products = lax.dot_general(
                known[known_id],
                reduced[reduced_id],
                (((1,), (1,)), ((), ())),
                preferred_element_type=jnp.float32,
            )
            scores = (products + spread[known_id]).reshape(TILE // 8, 8, TILE)
            peak = jnp.max(scores, axis=0)
            summed = jnp.sum(jnp.exp2((scores - peak[None]) * scale), axis=0)
            found.append((jnp.where(slot < count, reduced_id, dummy), peak, summed))
        return tuple(found)

    nothing = tuple(
        (jnp.int32(dummy), jnp.full((8, TILE), FLOOR, jnp.float32), jnp.zeros((8, TILE), jnp.float32))
        for lane in range(UNROLL)
    )
    merge(lax.fori_loop(0, (count + UNROLL - 1) // UNROLL, turn, nothing))
    top = peaks[0:dummy]
    peak = jnp.max(top, axis=1)
    summed = jnp.sum(sums[0:dummy] * jnp.exp2((top - peak[:, None, :]) * scale), axis=1)
    live = summed > 0.0
    out[...] = jnp.where(live, peak + jnp.log2(jnp.where(live, summed, 1.0)) / scale, FLOOR)


def finish_kernel(scale, to_unit, parts_count, *refs):
    parts, (aux, norms, out) = refs[:parts_count], refs[parts_count:]
    potential = aux[...] - merge_logs([part[...] for part in parts], scale)
    out[...] = (potential + norms[...]) / to_unit


def shards(
    source_embed, target_embed, source_mass, target_mass, target_start, tile_list, tile_count
):
    width = source_embed.shape[1]
    shard_count = lax.axis_size("src")
    half = shard_count // 2
    src_index = lax.axis_index("src")
    core = lax.axis_index("tgt")
    upper = src_index // half
    unit = 2.0 / (width * EPSILON)
    scale = unit * math.log2(math.e)
    to_unit = 0.5 * width

    source_blocks = source_embed.reshape(-1, TILE, width)
    target_blocks = target_embed.reshape(-1, TILE, width)
    src_rows = source_blocks.shape[0]
    own_cols = target_blocks.shape[0]
    col_blocks = own_cols * half
    chunks = math.gcd(CHUNKS, own_cols)
    chunk = own_cols // chunks
    side = src_rows // lax.axis_size("tgt")
    pieces = math.gcd(CHUNKS, side)
    piece = side // pieces

    meta = jnp.stack([upper, core, src_index % half]).astype(jnp.int32)

    counts = jnp.broadcast_to(tile_count.reshape(1, 1), (1, tile_list.shape[3]))
    own_list = jnp.concatenate([tile_list[0, 0], counts], axis=0).astype(jnp.int32)
    log_source = (jnp.log(source_mass) / unit).reshape(src_rows, TILE)
    log_target = (jnp.log(target_mass) / unit).reshape(-1, TILE)

    held = {0: [target_blocks[i * chunk : (i + 1) * chunk] for i in range(chunks)]}
    for slot in range(1, half):
        low = slot & -slot
        held[slot] = [hop(part, low) for part in held[slot ^ low]]
    share = lax.dynamic_slice_in_dim(source_blocks, core * side, side)
    direct = [hop(share[i * piece : (i + 1) * piece], half) for i in range(pieces)]
    swapped = [hop(part, 0, 1) for part in direct]

    peer_list = hop(own_list, half)
    peer_log = hop(log_source, half)

    smem = pl.BlockSpec(memory_space=pltpu.SMEM)
    vmem = pl.BlockSpec(memory_space=pltpu.VMEM)
    slots = 2 * tile_list.shape[3] + UNROLL
    tiles = pl.pallas_call(
        lambda *refs: list_kernel(src_rows, col_blocks, *refs),
        out_shape=[jax.ShapeDtypeStruct((size,), jnp.int32) for size in (slots, slots, 1)],
        in_specs=[smem] * 3,
        out_specs=[smem] * 3,
        name="tile_lists",
    )(meta, own_list, peer_list)

    def pair(mine, theirs):
        return jnp.where(upper == 0, jnp.concatenate([mine, theirs]), jnp.concatenate([theirs, mine]))

    log_pair = pair(log_source, peer_log)
    log_half = lax.dynamic_slice_in_dim(log_target, upper * col_blocks, col_blocks)
    start_half = lax.dynamic_slice_in_dim(
        target_start.reshape(-1, TILE), upper * col_blocks, col_blocks
    )
    slot_norms = jnp.stack(
        [jnp.concatenate([half_norms(part) for part in held[slot]]) for slot in range(half)]
    )
    order = jnp.arange(half) ^ (src_index % half)
    target_norms = slot_norms[order].reshape(col_blocks, TILE)
    source_norms = half_norms(source_blocks)
    start = start_half * to_unit - target_norms

    src_pieces, src_places = [source_blocks], [lambda meta: meta[0] * src_rows]
    for turn, group in enumerate((direct, swapped)):
        for i, part in enumerate(group):
            src_pieces.append(part)
            src_places.append(
                lambda meta, turn=turn, i=i: (1 - meta[0]) * src_rows
                + jnp.abs(meta[1] - turn) * side
                + i * piece
            )
    tgt_pieces, tgt_places = [], []
    for slot in range(half):
        for i, part in enumerate(held[slot]):
            tgt_pieces.append(part)
            tgt_places.append(
                lambda meta, slot=slot, i=i: (meta[2] ^ slot) * own_cols + i * chunk
            )

    def run(by_row, first, parts, aux, has_out):
        known, reduced = (col_blocks, 2 * src_rows) if by_row else (2 * src_rows, col_blocks)
        out_shape = [jax.ShapeDtypeStruct((reduced, TILE), jnp.float32)]
        if has_out:
            out_shape.append(jax.ShapeDtypeStruct((known, TILE), jnp.float32))
        anywhere = pl.BlockSpec(memory_space=pl.ANY)
        count = len(src_pieces) + len(tgt_pieces)
        results = pl.pallas_call(
            lambda *refs: pass_kernel(
                scale, by_row, first, (len(parts), src_places, tgt_places), has_out, *refs
            ),
            out_shape=out_shape,
            in_specs=[smem] * 4 + [vmem] * (len(parts) + 1) + [anywhere] * count,
            out_specs=[vmem] * len(out_shape),
            scratch_shapes=[
                pltpu.VMEM((2 * src_rows, TILE, width), jnp.bfloat16),
                pltpu.VMEM((col_blocks, TILE, width), jnp.bfloat16),
                pltpu.VMEM((known, TILE, TILE), jnp.float32),
                pltpu.VMEM((reduced + 1, 8, TILE), jnp.float32),
                pltpu.VMEM((reduced + 1, 8, TILE), jnp.float32),
                pltpu.SemaphoreType.DMA((count,)),
            ],
            compiler_params=pltpu.CompilerParams(vmem_limit_bytes=VMEM_LIMIT),
            name="row_pass" if by_row else "column_pass",
        )(meta, *tiles, *parts, aux, *src_pieces, *tgt_pieces)
        return results

    def share_rows(part):
        return [part, hop(part, 0, 1), hop(part, half), hop(part, half, 1)]

    def share_columns(part):
        return [part] + [hop(part, mask) for mask in range(1, half)]

    rows = run(True, True, [start], start, False)[0]
    columns = run(False, False, share_rows(rows), log_pair, False)[0]
    rows = run(True, False, share_columns(columns), log_half, False)[0]
    columns, source_final = run(False, False, share_rows(rows), log_pair, True)
    gathered = share_columns(columns)
    target_final = pl.pallas_call(
        lambda *refs: finish_kernel(scale, to_unit, len(gathered), *refs),
        out_shape=jax.ShapeDtypeStruct((col_blocks, TILE), jnp.float32),
        in_specs=[vmem] * (len(gathered) + 2),
        out_specs=vmem,
        name="finish",
    )(*gathered, log_half, target_norms)
    target_pot = pair(target_final, hop(target_final, half))
    own_final = lax.dynamic_slice_in_dim(source_final, upper * src_rows, src_rows)
    source_pot = (own_final + source_norms) / to_unit
    return (source_pot.reshape(-1), target_pot.reshape(-1))


def solution(mesh):
    return jax.shard_map(
        shards,
        mesh=mesh,
        in_specs=(
            P(("groups", "src"), None),
            P(("groups", "tgt", "src"), None),
            P(("groups", "src")),
            P(("groups", "tgt")),
            P(("groups", "tgt")),
            P(("groups", "src"), "tgt", None, None),
            P(("groups", "src"), "tgt"),
        ),
        out_specs=(P(("groups", "src")), P(("groups", "tgt"))),
        check_vma=False,
    )
```

profile of v0, /device:TPU:0, one launch (start us, length us, event | category | flops | bytes accessed | tf_op | source)
XLA Modules:
  0.0 109.8 jit_solution(15873360294662367910)
XLA Ops:
  0.7 1.2 %fusion.4 = (bf16[512,256]{1,0:T(8,128)(2,1)S(1)}, bf16[512,256]{1,0:T(8,128)(2,1)S(1)}) fusion(bf16[1024,256]{1,0:T(8,128)(2,1)} %param.8), kind=kLoop, calls=%fused_computation.39 | loop fusion | bytes 1048576 | tf_op jit(solution)/shard_map/slice | solution.py:182
  1.9 3.1 %collective-permute-start.4 = (bf16[4,128,256]{2,1,0:T(8,128)(2,1)S(1)}, bf16[4,128,256]{2,1,0:T(8,128)(2,1)S(1)}, u32[]{:S(2)}, u32[]{:S(2)}) collective-permute-start(bf16[4,128,256]{2,1,0:T(8,128)(2,1)S(1)} %bitcast.51), channel_id=1, source_target_pairs={{0,4},{1,5},{2,6},{3,7},{4,0},{5,1},{6,2},{7,3},{8,12},{9,13},{10,... | collective-permute-start | bytes 786440 | tf_op jit(solution)/shard_map/ppermute | solution.py:22
  4.9 1.5 %collective-permute-start.2 = (bf16[4,128,256]{2,1,0:T(8,128)(2,1)S(1)}, bf16[4,128,256]{2,1,0:T(8,128)(2,1)S(1)}, u32[]{:S(2)}, u32[]{:S(2)}) collective-permute-start(bf16[4,128,256]{2,1,0:T(8,128)(2,1)S(1)} %bitcast.52), channel_id=1, source_target_pairs={{0,2},{1,3},{2,0},{3,1},{4,6},{5,7},{6,4},{7,5},{8,10},{9,11},{10,... | collective-permute-start | bytes 786440 | tf_op jit(solution)/shard_map/ppermute | solution.py:22
  6.5 0.4 collective-permute-start.3
  6.9 0.1 collective-permute-start.1
  7.7 0.0 copy-start.13
  7.7 3.0 %collective-permute-start = (s32[3,128]{1,0:T(4,128)S(1)}, s32[3,128]{1,0:T(4,128)S(1)}, u32[]{:S(2)}, u32[]{:S(2)}) collective-permute-start(s32[3,128]{1,0:T(4,128)S(1)} %concatenate.27.refs_1_), channel_id=1, source_target_pairs={{0,8},{1,9},{2,10},{3,11},{4,12},{5,13},{6,14},{7,15},{8,0},{9,1},... | collective-permute-start | bytes 4616 | tf_op jit(solution)/shard_map/ppermute | solution.py:22
  10.8 0.2 multiply_reduce_fusion.8
  11.1 0.8 constant_dynamic-slice_fusion.2
  12.0 0.6 pad_add_fusion.refs_0_
  12.6 3.6 %collective-permute-done.refs_2_ = s32[3,128]{1,0:T(4,128)S(1)} collective-permute-done((s32[3,128]{1,0:T(4,128)S(1)}, s32[3,128]{1,0:T(4,128)S(1)}, u32[]{:S(2)}, u32[]{:S(2)}) %collective-permute-start) | collective-permute-done | bytes 1568 | tf_op jit(solution)/shard_map/ppermute | solution.py:22
  16.2 3.4 %collective-permute-start.8 = (bf16[4,128,256]{2,1,0:T(8,128)(2,1)}, bf16[4,128,256]{2,1,0:T(8,128)(2,1)S(1)}, u32[]{:S(2)}, u32[]{:S(2)}) collective-permute-start(bf16[4,128,256]{2,1,0:T(8,128)(2,1)} %get-tuple-element.14), channel_id=1, source_target_pairs={{0,8},{1,9},{2,10},{3,11},{4,12},{5,13},{6,14},{7,15},{8,0},{9,1},... | collective-permute-start | bytes 786440 | tf_op jit(solution)/shard_map/ppermute | solution.py:22
  19.6 4.3 %tile_lists.1 = (s32[260]{0:T(512)}, s32[260]{0:T(512)}, s32[1]{0:T(128)}) custom-call(s32[3]{0:T(128)} %pad_add_fusion.refs_0_, s32[3,128]{1,0:T(4,128)} %copy-done.13, s32[3,128]{1,0:T(4,128)} %copy-done.15), custom_call_target="tpu_custom_call" | custom-call | tf_op jit(solution)/shard_map/tile_lists/pallas_call | solution.py:196
  23.8 0.0 collective-permute-done.4.refs_16_.refs_19_
  23.9 0.6 collective-permute-start.7
  24.5 0.1 multiply_reduce_fusion.3
  24.6 0.0 collective-permute-done.3.refs_15_.refs_18_
  24.7 2.4 %collective-permute-start.14 = (f32[16,128]{1,0:T(8,128)S(1)}, f32[16,128]{1,0:T(8,128)S(1)}, u32[]{:S(2)}, u32[]{:S(2)}) collective-permute-start(f32[16,128]{1,0:T(8,128)S(1)} %multiply_bitcast_fusion.1), channel_id=1, source_target_pairs={{0,8},{1,9},{2,10},{3,11},{4,12},{5,13},{6,14},{7,15},{8,0},{9,1},... | collective-permute-start | bytes 24584 | tf_op jit(solution)/shard_map/ppermute | solution.py:22
  27.1 0.1 multiply_reduce_fusion.4
  27.2 0.0 collective-permute-done.2.refs_14_.refs_17_
  27.3 1.6 %collective-permute-start.6 = (bf16[4,128,256]{2,1,0:T(8,128)(2,1)S(1)}, bf16[4,128,256]{2,1,0:T(8,128)(2,1)S(1)}, u32[]{:S(2)}, u32[]{:S(2)}) collective-permute-start(bf16[4,128,256]{2,1,0:T(8,128)(2,1)S(1)} %collective-permute-done.4.refs_16_.refs_19_), channel_id=1, source_target_pairs={{0,2},{1,3},{2,0},{3,1},{4,6},{5,7},{6,4},{7,5},{8,10},{9,11},{10,... | collective-permute-start | bytes 786440 | tf_op jit(solution)/shard_map/ppermute | solution.py:22
  28.8 0.1 multiply_reduce_fusion.5
  29.0 0.6 collective-permute-start.5
  29.6 0.1 multiply_reduce_fusion.6
  29.7 8.7 %collective-permute-done.8.refs_8_.refs_11_ = bf16[4,128,256]{2,1,0:T(8,128)(2,1)S(1)} collective-permute-done((bf16[4,128,256]{2,1,0:T(8,128)(2,1)}, bf16[4,128,256]{2,1,0:T(8,128)(2,1)S(1)}, u32[]{:S(2)}, u32[]{:S(2)}) %collective-permute-start.8) | collective-permute-done | bytes 262176 | tf_op jit(solution)/shard_map/ppermute | solution.py:22
  38.4 0.0 collective-permute-start.10
  38.4 3.7 %collective-permute-done.7.refs_7_.refs_10_ = bf16[4,128,256]{2,1,0:T(8,128)(2,1)} collective-permute-done((bf16[4,128,256]{2,1,0:T(8,128)(2,1)}, bf16[4,128,256]{2,1,0:T(8,128)(2,1)}, u32[]{:S(2)}, u32[]{:S(2)}) %collective-permute-start.7) | collective-permute-done | bytes 262176 | tf_op jit(solution)/shard_map/ppermute | solution.py:22
  42.2 0.1 multiply_reduce_fusion.1
  42.3 0.0 collective-permute-done.5.refs_17_.refs_20_
  42.3 0.1 multiply_reduce_fusion.2
  42.5 0.6 gather_fusion
  43.1 0.9 collective-permute-done.9.refs_9_.refs_12_
  44.0 7.5 %row_pass.2.refs_4_ = f32[32,128]{1,0:T(8,128)S(1)} custom-call(s32[3]{0:T(128)S(1)} %copy-done.4, s32[260]{0:T(512)S(1)} %copy-done.2, s32[260]{0:T(512)S(1)} %copy-done.3, s32[1]{0:T(128)} %get-tuple-element.9.refs_3_, f32[32,128]{1,0:T(8,128)S(1)} %multiply_subtract_fusion.refs_4_.refs_5_, f32[32,128]{1,0:T(8,128)S(1)} %multiply_subtract_fusion.refs_4_.refs_5_, ...), custom_call_target="tpu_custom_call" | custom-call | tf_op jit(solution)/shard_map/row_pass/pallas_call | solution.py:244
  51.5 0.1 collective-permute-start.11
  51.6 0.1 collective-permute-start.12
  51.7 2.7 %collective-permute-start.13 = (f32[32,128]{1,0:T(8,128)S(1)}, f32[32,128]{1,0:T(8,128)S(1)}, u32[]{:S(2)}, u32[]{:S(2)}) collective-permute-start(f32[32,128]{1,0:T(8,128)S(1)} %row_pass.2.refs_4_), channel_id=1, source_target_pairs={{0,9},{1,8},{2,11},{3,10},{4,13},{5,12},{6,15},{7,14},{8,1},{9,0},... | collective-permute-start | bytes 49160 | tf_op jit(solution)/shard_map/ppermute | solution.py:22
  54.4 0.0 collective-permute-done.14
  54.4 1.9 %collective-permute-done.12.refs_6_ = f32[32,128]{1,0:T(8,128)S(1)} collective-permute-done((f32[32,128]{1,0:T(8,128)S(1)}, f32[32,128]{1,0:T(8,128)S(1)}, u32[]{:S(2)}, u32[]{:S(2)}) %collective-permute-start.12) | collective-permute-done | bytes 16416 | tf_op jit(solution)/shard_map/ppermute | solution.py:22
  56.3 0.0 collective-permute-done.13.refs_7_
  56.3 7.5 %column_pass.2.refs_4_ = f32[32,128]{1,0:T(8,128)S(1)} custom-call(s32[3]{0:T(128)S(1)} %copy-done.4, s32[260]{0:T(512)S(1)} %copy-done.2, s32[260]{0:T(512)S(1)} %copy-done.3, s32[1]{0:T(128)} %get-tuple-element.9.refs_3_, f32[32,128]{1,0:T(8,128)S(1)} %row_pass.2.refs_4_, f32[32,128]{1,0:T(8,128)S(1)} %collective-permute-done.11.refs_5_, ...), custom_call_target="tpu_custom_call" | custom-call | tf_op jit(solution)/shard_map/column_pass/pallas_call | solution.py:244
  63.8 4.3 %collective-permute-start.15 = (f32[32,128]{1,0:T(8,128)S(1)}, f32[32,128]{1,0:T(8,128)S(1)}, u32[]{:S(2)}, u32[]{:S(2)}) collective-permute-start(f32[32,128]{1,0:T(8,128)S(1)} %column_pass.2.refs_4_), channel_id=1, source_target_pairs={{0,2},{1,3},{2,0},{3,1},{4,6},{5,7},{6,4},{7,5},{8,10},{9,11},{10,... | collective-permute-start | bytes 49160 | tf_op jit(solution)/shard_map/ppermute | solution.py:22
  68.1 1.5 %collective-permute-start.17 = (f32[32,128]{1,0:T(8,128)S(1)}, f32[32,128]{1,0:T(8,128)S(1)}, u32[]{:S(2)}, u32[]{:S(2)}) collective-permute-start(f32[32,128]{1,0:T(8,128)S(1)} %column_pass.2.refs_4_), channel_id=1, source_target_pairs={{0,6},{1,7},{2,4},{3,5},{4,2},{5,3},{6,0},{7,1},{8,14},{9,15},{10,... | collective-permute-start | bytes 49160 | tf_op jit(solution)/shard_map/ppermute | solution.py:22
  69.7 0.2 collective-permute-done.15.refs_5_
  69.8 2.0 %collective-permute-done.16.refs_6_ = f32[32,128]{1,0:T(8,128)S(1)} collective-permute-done((f32[32,128]{1,0:T(8,128)S(1)}, f32[32,128]{1,0:T(8,128)S(1)}, u32[]{:S(2)}, u32[]{:S(2)}) %collective-permute-start.16) | collective-permute-done | bytes 16416 | tf_op jit(solution)/shard_map/ppermute | solution.py:22
  71.9 1.0 collective-permute-done.17.refs_7_
  72.8 7.5 %row_pass.3.refs_4_ = f32[32,128]{1,0:T(8,128)S(1)} custom-call(s32[3]{0:T(128)S(1)} %copy-done.4, s32[260]{0:T(512)S(1)} %copy-done.2, s32[260]{0:T(512)S(1)} %copy-done.3, s32[1]{0:T(128)} %get-tuple-element.9.refs_3_, f32[32,128]{1,0:T(8,128)S(1)} %column_pass.2.refs_4_, f32[32,128]{1,0:T(8,128)S(1)} %collective-permute-done.15.refs_5_, ...), custom_call_target="tpu_custom_call" | custom-call | tf_op jit(solution)/shard_map/row_pass/pallas_call | solution.py:244
  80.3 0.3 collective-permute-start.18
  80.6 0.0 collective-permute-start.19
  80.6 2.6 %collective-permute-start.20 = (f32[32,128]{1,0:T(8,128)S(1)}, f32[32,128]{1,0:T(8,128)S(1)}, u32[]{:S(2)}, u32[]{:S(2)}) collective-permute-start(f32[32,128]{1,0:T(8,128)S(1)} %row_pass.3.refs_4_), channel_id=1, source_target_pairs={{0,9},{1,8},{2,11},{3,10},{4,13},{5,12},{6,15},{7,14},{8,1},{9,0},... | collective-permute-start | bytes 49160 | tf_op jit(solution)/shard_map/ppermute | solution.py:22
  83.2 2.1 %collective-permute-done.19.refs_6_ = f32[32,128]{1,0:T(8,128)S(1)} collective-permute-done((f32[32,128]{1,0:T(8,128)S(1)}, f32[32,128]{1,0:T(8,128)S(1)}, u32[]{:S(2)}, u32[]{:S(2)}) %collective-permute-start.19) | collective-permute-done | bytes 16416 | tf_op jit(solution)/shard_map/ppermute | solution.py:22
  85.2 0.0 collective-permute-done.20.refs_7_
  85.2 7.5 %column_pass.3 = (f32[32,128]{1,0:T(8,128)S(1)}, f32[32,128]{1,0:T(8,128)S(1)}) custom-call(s32[3]{0:T(128)S(1)} %copy-done.4, s32[260]{0:T(512)S(1)} %copy-done.2, s32[260]{0:T(512)S(1)} %copy-done.3, s32[1]{0:T(128)} %get-tuple-element.9.refs_3_, f32[32,128]{1,0:T(8,128)S(1)} %row_pass.3.refs_4_, f32[32,128]{1,0:T(8,128)S(1)} %collective-permute-done.18.refs_5_, ...), custom_call_target="tpu_custom_call" | custom-call | tf_op jit(solution)/shard_map/column_pass/pallas_call | solution.py:244
  92.7 0.0 copy-start.5
  92.7 4.1 %collective-permute-start.21 = (f32[32,128]{1,0:T(8,128)S(1)}, f32[32,128]{1,0:T(8,128)S(1)}, u32[]{:S(2)}, u32[]{:S(2)}) collective-permute-start(f32[32,128]{1,0:T(8,128)S(1)} %get-tuple-element.11.refs_0_), channel_id=1, source_target_pairs={{0,2},{1,3},{2,0},{3,1},{4,6},{5,7},{6,4},{7,5},{8,10},{9,11},{10,... | collective-permute-start | bytes 49160 | tf_op jit(solution)/shard_map/ppermute | solution.py:22
  96.8 1.5 %collective-permute-start.23 = (f32[32,128]{1,0:T(8,128)S(1)}, f32[32,128]{1,0:T(8,128)S(1)}, u32[]{:S(2)}, u32[]{:S(2)}) collective-permute-start(f32[32,128]{1,0:T(8,128)S(1)} %get-tuple-element.11.refs_0_), channel_id=1, source_target_pairs={{0,6},{1,7},{2,4},{3,5},{4,2},{5,3},{6,0},{7,1},{8,14},{9,15},{10,... | collective-permute-start | bytes 49160 | tf_op jit(solution)/shard_map/ppermute | solution.py:22
  98.3 0.3 multiply_reduce_fusion
  98.7 0.0 collective-permute-done.21.refs_1_
  98.7 1.8 %collective-permute-done.22.refs_2_ = f32[32,128]{1,0:T(8,128)S(1)} collective-permute-done((f32[32,128]{1,0:T(8,128)S(1)}, f32[32,128]{1,0:T(8,128)S(1)}, u32[]{:S(2)}, u32[]{:S(2)}) %collective-permute-start.22) | collective-permute-done | bytes 16416 | tf_op jit(solution)/shard_map/ppermute | solution.py:22
  100.5 1.0 collective-permute-done.23.refs_3_
  101.5 0.6 copy-done.11
  102.1 1.4 %finish.1 = f32[32,128]{1,0:T(8,128)} custom-call(f32[32,128]{1,0:T(8,128)} %copy-done.5, f32[32,128]{1,0:T(8,128)} %copy-done.9, f32[32,128]{1,0:T(8,128)} %copy-done.10, f32[32,128]{1,0:T(8,128)} %copy-done.11, f32[32,128]{1,0:T(8,128)} %copy-done.1, f32[32,128]{1,0:T(8,128)} %bitcast.57), custom_call_target="tpu_custom_call" | custom-call | tf_op jit(solution)/shard_map/finish/pallas_call | solution.py:275
  103.6 0.6 fusion.2
  104.2 4.2 %collective-permute-done.24 = f32[32,128]{1,0:T(8,128)S(1)} collective-permute-done((f32[32,128]{1,0:T(8,128)}, f32[32,128]{1,0:T(8,128)S(1)}, u32[]{:S(2)}, u32[]{:S(2)}) %collective-permute-start.24) | collective-permute-done | bytes 16416 | tf_op jit(solution)/shard_map/ppermute | solution.py:22
  108.4 1.4 %fusion = f32[8192]{0:T(1024)} fusion(f32[32,128]{1,0:T(8,128)S(1)} %collective-permute-done.24, f32[32,128]{1,0:T(8,128)} %finish.1, pred[]{:T(512)S(6)} %eq.7), kind=kLoop, calls=%fused_computation.11 | loop fusion | flops 24576 | bytes 65537 | tf_op jit(solution)/shard_map/jit(_where)/select_n | solution.py:205
  (59 shorter events, 0.2 us)
Async XLA Ops:
  0.6 10.1 %copy-start.6 = (bf16[1024,256]{1,0:T(8,128)(2,1)S(1)}, bf16[1024,256]{1,0:T(8,128)(2,1)}, u32[]{:S(2)}) copy-start(bf16[1024,256]{1,0:T(8,128)(2,1)} %param.8) | copy-start | bytes 1572868
  0.6 7.1 %copy-start.16 = (s32[1,1,2,128]{3,2,1,0:T(2,128)S(1)}, s32[1,1,2,128]{3,2,1,0:T(2,128)}, u32[]{:S(2)}) copy-start(s32[1,1,2,128]{3,2,1,0:T(2,128)} %param.12) | copy-start | bytes 3076
  0.7 10.4 %copy-start.14 = (f32[2048]{0:T(1024)S(1)}, f32[2048]{0:T(1024)}, u32[]{:S(2)}) copy-start(f32[2048]{0:T(1024)} %param.9) | copy-start | bytes 24580
  0.7 10.4 %copy-start.8 = (f32[8192]{0:T(1024)S(1)}, f32[8192]{0:T(1024)}, u32[]{:S(2)}) copy-start(f32[8192]{0:T(1024)} %param.10) | copy-start | bytes 98308
  0.7 10.5 %copy-start = (bf16[2048,256]{1,0:T(8,128)(2,1)S(1)}, bf16[2048,256]{1,0:T(8,128)(2,1)}, u32[]{:S(2)}) copy-start(bf16[2048,256]{1,0:T(8,128)(2,1)} %param.7) | copy-start | bytes 3145732
  1.9 22.0 %collective-permute-start.4 = (bf16[4,128,256]{2,1,0:T(8,128)(2,1)S(1)}, bf16[4,128,256]{2,1,0:T(8,128)(2,1)S(1)}, u32[]{:S(2)}, u32[]{:S(2)}) collective-permute-start(bf16[4,128,256]{2,1,0:T(8,128)(2,1)S(1)} %bitcast.51), channel_id=1, source_target_pairs={{0,4},{1,5},{2,6},{3,7},{4,0},{5,1},{6,2},{7,3},{8,12},{9,13},{10,... | collective-permute-start | bytes 786440 | tf_op jit(solution)/shard_map/ppermute | solution.py:22
  4.9 22.3 %collective-permute-start.2 = (bf16[4,128,256]{2,1,0:T(8,128)(2,1)S(1)}, bf16[4,128,256]{2,1,0:T(8,128)(2,1)S(1)}, u32[]{:S(2)}, u32[]{:S(2)}) collective-permute-start(bf16[4,128,256]{2,1,0:T(8,128)(2,1)S(1)} %bitcast.52), channel_id=1, source_target_pairs={{0,2},{1,3},{2,0},{3,1},{4,6},{5,7},{6,4},{7,5},{8,10},{9,11},{10,... | collective-permute-start | bytes 786440 | tf_op jit(solution)/shard_map/ppermute | solution.py:22
  6.5 18.2 %collective-permute-start.3 = (bf16[4,128,256]{2,1,0:T(8,128)(2,1)S(1)}, bf16[4,128,256]{2,1,0:T(8,128)(2,1)S(1)}, u32[]{:S(2)}, u32[]{:S(2)}) collective-permute-start(bf16[4,128,256]{2,1,0:T(8,128)(2,1)S(1)} %bitcast.45), channel_id=1, source_target_pairs={{0,4},{1,5},{2,6},{3,7},{4,0},{5,1},{6,2},{7,3},{8,12},{9,13},{10,... | collective-permute-start | bytes 786440 | tf_op jit(solution)/shard_map/ppermute | solution.py:22
  6.9 22.1 %collective-permute-start.1 = (bf16[4,128,256]{2,1,0:T(8,128)(2,1)S(1)}, bf16[4,128,256]{2,1,0:T(8,128)(2,1)S(1)}, u32[]{:S(2)}, u32[]{:S(2)}) collective-permute-start(bf16[4,128,256]{2,1,0:T(8,128)(2,1)S(1)} %bitcast.46), channel_id=1, source_target_pairs={{0,2},{1,3},{2,0},{3,1},{4,6},{5,7},{6,4},{7,5},{8,10},{9,11},{10,... | collective-permute-start | bytes 786440 | tf_op jit(solution)/shard_map/ppermute | solution.py:22
  7.7 11.8 %copy-start.13 = (s32[3,128]{1,0:T(4,128)}, s32[3,128]{1,0:T(4,128)S(1)}, u32[]{:S(2)}) copy-start(s32[3,128]{1,0:T(4,128)S(1)} %concatenate.27.refs_1_) | copy-start | bytes 4612
  7.7 8.4 %collective-permute-start = (s32[3,128]{1,0:T(4,128)S(1)}, s32[3,128]{1,0:T(4,128)S(1)}, u32[]{:S(2)}, u32[]{:S(2)}) collective-permute-start(s32[3,128]{1,0:T(4,128)S(1)} %concatenate.27.refs_1_), channel_id=1, source_target_pairs={{0,8},{1,9},{2,10},{3,11},{4,12},{5,13},{6,14},{7,15},{8,0},{9,1},... | collective-permute-start | bytes 4616 | tf_op jit(solution)/shard_map/ppermute | solution.py:22
  12.0 31.1 %copy-start.12 = (f32[8192]{0:T(1024)S(1)}, f32[8192]{0:T(1024)}, u32[]{:S(2)}) copy-start(f32[8192]{0:T(1024)} %param.11) | copy-start | bytes 98308
  12.6 31.4 %copy-start.4 = (s32[3]{0:T(128)S(1)}, s32[3]{0:T(128)}, u32[]{:S(2)}) copy-start(s32[3]{0:T(128)} %pad_add_fusion.refs_0_) | copy-start | bytes 40
  16.2 3.4 %copy-start.15 = (s32[3,128]{1,0:T(4,128)}, s32[3,128]{1,0:T(4,128)S(1)}, u32[]{:S(2)}) copy-start(s32[3,128]{1,0:T(4,128)S(1)} %collective-permute-done.refs_2_) | copy-start | bytes 4612
  16.2 22.2 %collective-permute-start.8 = (bf16[4,128,256]{2,1,0:T(8,128)(2,1)}, bf16[4,128,256]{2,1,0:T(8,128)(2,1)S(1)}, u32[]{:S(2)}, u32[]{:S(2)}) collective-permute-start(bf16[4,128,256]{2,1,0:T(8,128)(2,1)} %get-tuple-element.14), channel_id=1, source_target_pairs={{0,8},{1,9},{2,10},{3,11},{4,12},{5,13},{6,14},{7,15},{8,0},{9,1},... | collective-permute-start | bytes 786440 | tf_op jit(solution)/shard_map/ppermute | solution.py:22
  23.8 20.2 %copy-start.2 = (s32[260]{0:T(512)S(1)}, s32[260]{0:T(512)}, u32[]{:S(2)}) copy-start(s32[260]{0:T(512)} %get-tuple-element.7.refs_1_) | copy-start | bytes 3124
  23.8 20.2 %copy-start.3 = (s32[260]{0:T(512)S(1)}, s32[260]{0:T(512)}, u32[]{:S(2)}) copy-start(s32[260]{0:T(512)} %get-tuple-element.8.refs_2_) | copy-start | bytes 3124
  23.9 18.3 %collective-permute-start.7 = (bf16[4,128,256]{2,1,0:T(8,128)(2,1)}, bf16[4,128,256]{2,1,0:T(8,128)(2,1)}, u32[]{:S(2)}, u32[]{:S(2)}) collective-permute-start(bf16[4,128,256]{2,1,0:T(8,128)(2,1)} %get-tuple-element.15), channel_id=1, source_target_pairs={{0,8},{1,9},{2,10},{3,11},{4,12},{5,13},{6,14},{7,15},{8,0},{9,1},... | collective-permute-start | bytes 786440 | tf_op jit(solution)/shard_map/ppermute | solution.py:22
  24.7 29.7 %collective-permute-start.14 = (f32[16,128]{1,0:T(8,128)S(1)}, f32[16,128]{1,0:T(8,128)S(1)}, u32[]{:S(2)}, u32[]{:S(2)}) collective-permute-start(f32[16,128]{1,0:T(8,128)S(1)} %multiply_bitcast_fusion.1), channel_id=1, source_target_pairs={{0,8},{1,9},{2,10},{3,11},{4,12},{5,13},{6,14},{7,15},{8,0},{9,1},... | collective-permute-start | bytes 24584 | tf_op jit(solution)/shard_map/ppermute | solution.py:22
  27.3 14.9 %collective-permute-start.6 = (bf16[4,128,256]{2,1,0:T(8,128)(2,1)S(1)}, bf16[4,128,256]{2,1,0:T(8,128)(2,1)S(1)}, u32[]{:S(2)}, u32[]{:S(2)}) collective-permute-start(bf16[4,128,256]{2,1,0:T(8,128)(2,1)S(1)} %collective-permute-done.4.refs_16_.refs_19_), channel_id=1, source_target_pairs={{0,2},{1,3},{2,0},{3,1},{4,6},{5,7},{6,4},{7,5},{8,10},{9,11},{10,... | collective-permute-start | bytes 786440 | tf_op jit(solution)/shard_map/ppermute | solution.py:22
  29.0 13.3 %collective-permute-start.5 = (bf16[4,128,256]{2,1,0:T(8,128)(2,1)S(1)}, bf16[4,128,256]{2,1,0:T(8,128)(2,1)S(1)}, u32[]{:S(2)}, u32[]{:S(2)}) collective-permute-start(bf16[4,128,256]{2,1,0:T(8,128)(2,1)S(1)} %collective-permute-done.3.refs_15_.refs_18_), channel_id=1, source_target_pairs={{0,2},{1,3},{2,0},{3,1},{4,6},{5,7},{6,4},{7,5},{8,10},{9,11},{10,... | collective-permute-start | bytes 786440 | tf_op jit(solution)/shard_map/ppermute | solution.py:22
  38.4 4.7 %collective-permute-start.10 = (bf16[4,128,256]{2,1,0:T(8,128)(2,1)S(1)}, bf16[4,128,256]{2,1,0:T(8,128)(2,1)}, u32[]{:S(2)}, u32[]{:S(2)}) collective-permute-start(bf16[4,128,256]{2,1,0:T(8,128)(2,1)S(1)} %collective-permute-done.8.refs_8_.refs_11_), channel_id=1, source_target_pairs={{0,1},{1,0},{2,3},{3,2},{4,5},{5,4},{6,7},{7,6},{8,9},{9,8},{10,11... | collective-permute-start | bytes 786440 | tf_op jit(solution)/shard_map/ppermute | solution.py:22
  42.1 1.9 %collective-permute-start.9 = (bf16[4,128,256]{2,1,0:T(8,128)(2,1)}, bf16[4,128,256]{2,1,0:T(8,128)(2,1)}, u32[]{:S(2)}, u32[]{:S(2)}) collective-permute-start(bf16[4,128,256]{2,1,0:T(8,128)(2,1)} %collective-permute-done.7.refs_7_.refs_10_), channel_id=1, source_target_pairs={{0,1},{1,0},{2,3},{3,2},{4,5},{5,4},{6,7},{7,6},{8,9},{9,8},{10,11... | collective-permute-start | bytes 786440 | tf_op jit(solution)/shard_map/ppermute | solution.py:22
  43.1 8.4 %copy-start.7 = (f32[4,8,128]{2,1,0:T(8,128)}, f32[4,8,128]{2,1,0:T(8,128)S(1)}, u32[]{:S(2)}) copy-start(f32[4,8,128]{2,1,0:T(8,128)S(1)} %gather_fusion) | copy-start | bytes 49156
  51.5 2.9 %collective-permute-start.11 = (f32[32,128]{1,0:T(8,128)S(1)}, f32[32,128]{1,0:T(8,128)S(1)}, u32[]{:S(2)}, u32[]{:S(2)}) collective-permute-start(f32[32,128]{1,0:T(8,128)S(1)} %row_pass.2.refs_4_), channel_id=1, source_target_pairs={{0,1},{1,0},{2,3},{3,2},{4,5},{5,4},{6,7},{7,6},{8,9},{9,8},{10,11... | collective-permute-start | bytes 49160 | tf_op jit(solution)/shard_map/ppermute | solution.py:22
  51.6 4.7 %collective-permute-start.12 = (f32[32,128]{1,0:T(8,128)S(1)}, f32[32,128]{1,0:T(8,128)S(1)}, u32[]{:S(2)}, u32[]{:S(2)}) collective-permute-start(f32[32,128]{1,0:T(8,128)S(1)} %row_pass.2.refs_4_), channel_id=1, source_target_pairs={{0,8},{1,9},{2,10},{3,11},{4,12},{5,13},{6,14},{7,15},{8,0},{9,1},... | collective-permute-start | bytes 49160 | tf_op jit(solution)/shard_map/ppermute | solution.py:22
  51.7 4.6 %collective-permute-start.13 = (f32[32,128]{1,0:T(8,128)S(1)}, f32[32,128]{1,0:T(8,128)S(1)}, u32[]{:S(2)}, u32[]{:S(2)}) collective-permute-start(f32[32,128]{1,0:T(8,128)S(1)} %row_pass.2.refs_4_), channel_id=1, source_target_pairs={{0,9},{1,8},{2,11},{3,10},{4,13},{5,12},{6,15},{7,14},{8,1},{9,0},... | collective-permute-start | bytes 49160 | tf_op jit(solution)/shard_map/ppermute | solution.py:22
  63.8 6.0 %collective-permute-start.15 = (f32[32,128]{1,0:T(8,128)S(1)}, f32[32,128]{1,0:T(8,128)S(1)}, u32[]{:S(2)}, u32[]{:S(2)}) collective-permute-start(f32[32,128]{1,0:T(8,128)S(1)} %column_pass.2.refs_4_), channel_id=1, source_target_pairs={{0,2},{1,3},{2,0},{3,1},{4,6},{5,7},{6,4},{7,5},{8,10},{9,11},{10,... | collective-permute-start | bytes 49160 | tf_op jit(solution)/shard_map/ppermute | solution.py:22
  68.1 3.7 %collective-permute-start.16 = (f32[32,128]{1,0:T(8,128)S(1)}, f32[32,128]{1,0:T(8,128)S(1)}, u32[]{:S(2)}, u32[]{:S(2)}) collective-permute-start(f32[32,128]{1,0:T(8,128)S(1)} %column_pass.2.refs_4_), channel_id=1, source_target_pairs={{0,4},{1,5},{2,6},{3,7},{4,0},{5,1},{6,2},{7,3},{8,12},{9,13},{10,... | collective-permute-start | bytes 49160 | tf_op jit(solution)/shard_map/ppermute | solution.py:22
  68.1 4.7 %collective-permute-start.17 = (f32[32,128]{1,0:T(8,128)S(1)}, f32[32,128]{1,0:T(8,128)S(1)}, u32[]{:S(2)}, u32[]{:S(2)}) collective-permute-start(f32[32,128]{1,0:T(8,128)S(1)} %column_pass.2.refs_4_), channel_id=1, source_target_pairs={{0,6},{1,7},{2,4},{3,5},{4,2},{5,3},{6,0},{7,1},{8,14},{9,15},{10,... | collective-permute-start | bytes 49160 | tf_op jit(solution)/shard_map/ppermute | solution.py:22
  69.7 10.7 %copy-start.1 = (f32[32,128]{1,0:T(8,128)}, f32[32,128]{1,0:T(8,128)S(1)}, u32[]{:S(2)}) copy-start(f32[32,128]{1,0:T(8,128)S(1)} %constant_dynamic-slice_fusion.1.refs_8_.refs_4_) | copy-start | bytes 49156
  80.3 2.8 %collective-permute-start.18 = (f32[32,128]{1,0:T(8,128)S(1)}, f32[32,128]{1,0:T(8,128)S(1)}, u32[]{:S(2)}, u32[]{:S(2)}) collective-permute-start(f32[32,128]{1,0:T(8,128)S(1)} %row_pass.3.refs_4_), channel_id=1, source_target_pairs={{0,1},{1,0},{2,3},{3,2},{4,5},{5,4},{6,7},{7,6},{8,9},{9,8},{10,11... | collective-permute-start | bytes 49160 | tf_op jit(solution)/shard_map/ppermute | solution.py:22
  80.6 4.6 %collective-permute-start.19 = (f32[32,128]{1,0:T(8,128)S(1)}, f32[32,128]{1,0:T(8,128)S(1)}, u32[]{:S(2)}, u32[]{:S(2)}) collective-permute-start(f32[32,128]{1,0:T(8,128)S(1)} %row_pass.3.refs_4_), channel_id=1, source_target_pairs={{0,8},{1,9},{2,10},{3,11},{4,12},{5,13},{6,14},{7,15},{8,0},{9,1},... | collective-permute-start | bytes 49160 | tf_op jit(solution)/shard_map/ppermute | solution.py:22
  80.6 4.6 %collective-permute-start.20 = (f32[32,128]{1,0:T(8,128)S(1)}, f32[32,128]{1,0:T(8,128)S(1)}, u32[]{:S(2)}, u32[]{:S(2)}) collective-permute-start(f32[32,128]{1,0:T(8,128)S(1)} %row_pass.3.refs_4_), channel_id=1, source_target_pairs={{0,9},{1,8},{2,11},{3,10},{4,13},{5,12},{6,15},{7,14},{8,1},{9,0},... | collective-permute-start | bytes 49160 | tf_op jit(solution)/shard_map/ppermute | solution.py:22
  92.7 8.8 %copy-start.5 = (f32[32,128]{1,0:T(8,128)}, f32[32,128]{1,0:T(8,128)S(1)}, u32[]{:S(2)}) copy-start(f32[32,128]{1,0:T(8,128)S(1)} %get-tuple-element.11.refs_0_) | copy-start | bytes 49156
  92.7 6.0 %collective-permute-start.21 = (f32[32,128]{1,0:T(8,128)S(1)}, f32[32,128]{1,0:T(8,128)S(1)}, u32[]{:S(2)}, u32[]{:S(2)}) collective-permute-start(f32[32,128]{1,0:T(8,128)S(1)} %get-tuple-element.11.refs_0_), channel_id=1, source_target_pairs={{0,2},{1,3},{2,0},{3,1},{4,6},{5,7},{6,4},{7,5},{8,10},{9,11},{10,... | collective-permute-start | bytes 49160 | tf_op jit(solution)/shard_map/ppermute | solution.py:22
  96.8 3.7 %collective-permute-start.22 = (f32[32,128]{1,0:T(8,128)S(1)}, f32[32,128]{1,0:T(8,128)S(1)}, u32[]{:S(2)}, u32[]{:S(2)}) collective-permute-start(f32[32,128]{1,0:T(8,128)S(1)} %get-tuple-element.11.refs_0_), channel_id=1, source_target_pairs={{0,4},{1,5},{2,6},{3,7},{4,0},{5,1},{6,2},{7,3},{8,12},{9,13},{10,... | collective-permute-start | bytes 49160 | tf_op jit(solution)/shard_map/ppermute | solution.py:22
  96.8 4.7 %collective-permute-start.23 = (f32[32,128]{1,0:T(8,128)S(1)}, f32[32,128]{1,0:T(8,128)S(1)}, u32[]{:S(2)}, u32[]{:S(2)}) collective-permute-start(f32[32,128]{1,0:T(8,128)S(1)} %get-tuple-element.11.refs_0_), channel_id=1, source_target_pairs={{0,6},{1,7},{2,4},{3,5},{4,2},{5,3},{6,0},{7,1},{8,14},{9,15},{10,... | collective-permute-start | bytes 49160 | tf_op jit(solution)/shard_map/ppermute | solution.py:22
  98.7 2.8 %copy-start.9 = (f32[32,128]{1,0:T(8,128)}, f32[32,128]{1,0:T(8,128)S(1)}, u32[]{:S(2)}) copy-start(f32[32,128]{1,0:T(8,128)S(1)} %collective-permute-done.21.refs_1_) | copy-start | bytes 49156
  100.5 1.0 copy-start.10
  101.5 0.6 copy-start.11
  103.6 4.8 %collective-permute-start.24 = (f32[32,128]{1,0:T(8,128)}, f32[32,128]{1,0:T(8,128)S(1)}, u32[]{:S(2)}, u32[]{:S(2)}) collective-permute-start(f32[32,128]{1,0:T(8,128)} %finish.1), channel_id=1, source_target_pairs={{0,8},{1,9},{2,10},{3,11},{4,12},{5,13},{6,14},{7,15},{8,0},{9,1},... | collective-permute-start | bytes 49160 | tf_op jit(solution)/shard_map/ppermute | solution.py:22
where the time goes:
time: 109 us; the launch traced here: 110 us
  Pallas kernels  35.6 us (33%)
  starting transfers between devices  33.9 us (31%)
  waiting for transfers between devices  31.1 us (29%)
  other arithmetic  4.17 us (4%)
  local copies, waits for them, and re-layouts  3.22 us (3%)
  between operations  1.76 us (2%)
    ppermute x25, starting transfers between devices, hop(): lax.ppermute(value, ('src', 'tgt'), [(i, i ^ flip) for i in range(total)])  33.9 us
    ppermute x25, waiting for transfers between devices, hop(): lax.ppermute(value, ('src', 'tgt'), [(i, i ^ flip) for i in range(total)])  31.1 us
    pallas_call x4, Pallas kernels, run(): pl.pallas_call(lambda *refs: pass_kernel(scale, by_row, first, (len(parts...  29.9 us
    pallas_call x1, Pallas kernels, shards(): pl.pallas_call(lambda *refs: list_kernel(src_rows, col_blocks, *refs), ou...  4.25 us
  transfers between devices with their start and end apart: 25, of which 12 were waited for; matrix products, arithmetic and copies ran while one was open for 4% of the time, Pallas kernels for 11%

commit v1 on v0

--- a/solution.py
+++ b/solution.py
@@ -10,9 +10,9 @@
 TILE = 128
 EPSILON = 0.05
 FLOOR = -1e30
-UNROLL = 4
+UNROLL = 8
 CHUNKS = 2
-VMEM_LIMIT = 48 * 1024 * 1024
+VMEM_LIMIT = 6 * 1024 * 1024
 
 
 def hop(value, src_mask, tgt_mask=0):
@@ -62,28 +62,42 @@
     return peak + jnp.log2(summed) / scale
 
 
-def pass_kernel(
-    scale, by_row, first, places, has_out, meta, rows, cols, total, *refs
-):
-    n_parts, n_src, n_tgt = places
-    parts, refs = refs[:n_parts], refs[n_parts:]
-    aux, refs = refs[0], refs[1:]
+def product_kernel(places, meta, rows, cols, total, *refs):
+    n_src, n_tgt = places
     src_pieces, refs = refs[: len(n_src)], refs[len(n_src) :]
     tgt_pieces, refs = refs[: len(n_tgt)], refs[len(n_tgt) :]
-    out, refs = refs[0], refs[1:]
+    by_col, by_row, src, tgt, sems = refs
+    moves = []
+    for pieces, places_of, held in ((src_pieces, n_src, src), (tgt_pieces, n_tgt, tgt)):
+        for ref, place in zip(pieces, places_of):
+            start = pl.multiple_of(place(meta), ref.shape[0])
+            moves.append(
+                pltpu.make_async_copy(ref, held.at[pl.ds(start, ref.shape[0])], sems.at[len(moves)])
+            )
+    for move in moves:
+        move.start()
+    for move in moves:
+        move.wait()
+
+    def turn(index, carry):
+        for lane in range(UNROLL):
+            slot = index * UNROLL + lane
+            x, y = src[rows[slot]], tgt[cols[slot]]
+            for left, right, out in ((y, x, by_col), (x, y, by_row)):
+                out[slot] = lax.dot_general(
+                    left, right, (((1,), (1,)), ((), ())), preferred_element_type=jnp.float32
+                )
+        return carry
+
+    lax.fori_loop(0, (total[0] + UNROLL - 1) // UNROLL, turn, 0)
+
+
+def pass_kernel(scale, n_parts, first, has_out, known_ids, reduced_ids, total, *refs):
+    parts, refs = refs[:n_parts], refs[n_parts:]
+    aux, products, out, refs = refs[0], refs[1], refs[2], refs[3:]
     if has_out:
         extra, refs = refs[0], refs[1:]
-    src, tgt, spread, peaks, sums, sems = refs
-    copies = []
-    for ref, place in zip(src_pieces, n_src):
-        start = pl.multiple_of(place(meta), ref.shape[0])
-        copies.append((ref, src.at[pl.ds(start, ref.shape[0])]))
-    for ref, place in zip(tgt_pieces, n_tgt):
-        start = pl.multiple_of(place(meta), ref.shape[0])
-        copies.append((ref, tgt.at[pl.ds(start, ref.shape[0])]))
-    moves = [pltpu.make_async_copy(a, b, sems.at[i]) for i, (a, b) in enumerate(copies)]
-    for move in moves:
-        move.start()
+    spread, peaks, sums = refs
     peaks[...] = jnp.full(peaks.shape, FLOOR, jnp.float32)
     sums[...] = jnp.zeros(sums.shape, jnp.float32)
     if first:
@@ -95,10 +109,6 @@
     turned = jnp.transpose(potential)
     for block in range(potential.shape[0]):
         spread[block] = jnp.broadcast_to(turned[:, block : block + 1], (TILE, TILE))
-    for move in moves:
-        move.wait()
-    known, reduced = (tgt, src) if by_row else (src, tgt)
-    known_ids, reduced_ids = (cols, rows) if by_row else (rows, cols)
     dummy = peaks.shape[0] - 1
     count = total[0]
 
@@ -117,17 +127,10 @@
         found = []
         for lane in range(UNROLL):
             slot = index * UNROLL + lane
-            known_id, reduced_id = known_ids[slot], reduced_ids[slot]
-            products = lax.dot_general(
-                known[known_id],
-                reduced[reduced_id],
-                (((1,), (1,)), ((), ())),
-                preferred_element_type=jnp.float32,
-            )
-            scores = (products + spread[known_id]).reshape(TILE // 8, 8, TILE)
+            scores = (products[slot] + spread[known_ids[slot]]).reshape(TILE // 8, 8, TILE)
             peak = jnp.max(scores, axis=0)
             summed = jnp.sum(jnp.exp2((scores - peak[None]) * scale), axis=0)
-            found.append((jnp.where(slot < count, reduced_id, dummy), peak, summed))
+            found.append((jnp.where(slot < count, reduced_ids[slot], dummy), peak, summed))
         return tuple(found)
 
     nothing = tuple(
@@ -198,6 +201,7 @@
         out_shape=[jax.ShapeDtypeStruct((size,), jnp.int32) for size in (slots, slots, 1)],
         in_specs=[smem] * 3,
         out_specs=[smem] * 3,
+        compiler_params=pltpu.CompilerParams(vmem_limit_bytes=VMEM_LIMIT),
         name="tile_lists",
     )(meta, own_list, peer_list)
 
@@ -234,32 +238,42 @@
                 lambda meta, slot=slot, i=i: (meta[2] ^ slot) * own_cols + i * chunk
             )
 
-    def run(by_row, first, parts, aux, has_out):
-        known, reduced = (col_blocks, 2 * src_rows) if by_row else (2 * src_rows, col_blocks)
+    anywhere = pl.BlockSpec(memory_space=pl.ANY)
+    pieces_all = src_pieces + tgt_pieces
+    by_col, by_row = pl.pallas_call(
+        lambda *refs: product_kernel((src_places, tgt_places), *refs),
+        out_shape=[jax.ShapeDtypeStruct((slots, TILE, TILE), jnp.float32)] * 2,
+        in_specs=[smem] * 4 + [anywhere] * len(pieces_all),
+        out_specs=[vmem] * 2,
+        scratch_shapes=[
+            pltpu.VMEM((2 * src_rows, TILE, width), jnp.bfloat16),
+            pltpu.VMEM((col_blocks, TILE, width), jnp.bfloat16),
+            pltpu.SemaphoreType.DMA((len(pieces_all),)),
+        ],
+        compiler_params=pltpu.CompilerParams(vmem_limit_bytes=VMEM_LIMIT),
+        name="products",
+    )(meta, *tiles, *pieces_all)
+
+    def run(row_pass, first, parts, aux, has_out):
+        known, reduced = (col_blocks, 2 * src_rows) if row_pass else (2 * src_rows, col_blocks)
         out_shape = [jax.ShapeDtypeStruct((reduced, TILE), jnp.float32)]
         if has_out:
             out_shape.append(jax.ShapeDtypeStruct((known, TILE), jnp.float32))
-        anywhere = pl.BlockSpec(memory_space=pl.ANY)
-        count = len(src_pieces) + len(tgt_pieces)
-        results = pl.pallas_call(
-            lambda *refs: pass_kernel(
-                scale, by_row, first, (len(parts), src_places, tgt_places), has_out, *refs
-            ),
+        rows, cols, total = tiles
+        ids = (cols, rows) if row_pass else (rows, cols)
+        return pl.pallas_call(
+            lambda *refs: pass_kernel(scale, len(parts), first, has_out, *refs),
             out_shape=out_shape,
-            in_specs=[smem] * 4 + [vmem] * (len(parts) + 1) + [anywhere] * count,
+            in_specs=[smem] * 3 + [vmem] * (len(parts) + 2),
             out_specs=[vmem] * len(out_shape),
             scratch_shapes=[
-                pltpu.VMEM((2 * src_rows, TILE, width), jnp.bfloat16),
-                pltpu.VMEM((col_blocks, TILE, width), jnp.bfloat16),
                 pltpu.VMEM((known, TILE, TILE), jnp.float32),
                 pltpu.VMEM((reduced + 1, 8, TILE), jnp.float32),
                 pltpu.VMEM((reduced + 1, 8, TILE), jnp.float32),
-                pltpu.SemaphoreType.DMA((count,)),
             ],
             compiler_params=pltpu.CompilerParams(vmem_limit_bytes=VMEM_LIMIT),
-            name="row_pass" if by_row else "column_pass",
-        )(meta, *tiles, *parts, aux, *src_pieces, *tgt_pieces)
-        return results
+            name="row_pass" if row_pass else "column_pass",
+        )(*ids, total, *parts, aux, by_col if row_pass else by_row)
 
     def share_rows(part):
         return [part, hop(part, 0, 1), hop(part, half), hop(part, half, 1)]
@@ -277,6 +291,7 @@
         out_shape=jax.ShapeDtypeStruct((col_blocks, TILE), jnp.float32),
         in_specs=[vmem] * (len(gathered) + 2),
         out_specs=vmem,
+        compiler_params=pltpu.CompilerParams(vmem_limit_bytes=VMEM_LIMIT),
         name="finish",
     )(*gathered, log_half, target_norms)
     target_pot = pair(target_final, hop(target_final, half))

time: 109 us -> 97.6 us (0.90); the launches traced: 110 us -> 95.8 us
  Pallas kernels: 35.6 us -> 23.4 us
  waiting for transfers between devices: 31.1 us -> 27.5 us
  other arithmetic: 4.17 us -> 6.05 us
  local copies, waits for them, and re-layouts: 3.22 us -> 4.6 us
  starting transfers between devices: 33.9 us -> 32.7 us
    pallas_call x4 -> x5, Pallas kernels: 29.9 us -> 19.3 us  [the longest x4 13.7 us: run(): pl.pallas_call(lambda *refs: pass_kernel(scale, len(parts), first, has_ou...]
    ppermute x25, waiting for transfers between devices: 31.1 us -> 27.5 us  [hop(): lax.ppermute(value, ('src', 'tgt'), [(i, i ^ flip) for i in range(total)])]
    pallas_call x1, Pallas kernels: 1.44 us -> 0.03 us  [shards(): pl.pallas_call(lambda *refs: finish_kernel(scale, to_unit, len(gathered),...]
    ppermute x25, starting transfers between devices: 33.9 us -> 32.7 us  [hop(): lax.ppermute(value, ('src', 'tgt'), [(i, i ^ flip) for i in range(total)])]
  transfers between devices with their start and end apart: 25 -> 25, of which waited for: 12 -> 12; matrix products, arithmetic and copies ran while one was open for 4% -> 8% of each run, Pallas kernels for 11% -> 14%
where the time goes in v1:
time: 97.6 us; the launch traced here: 95.8 us
  starting transfers between devices  32.7 us (34%)
  waiting for transfers between devices  27.5 us (28%)
  Pallas kernels  23.4 us (24%)
  other arithmetic  6.05 us (6%)
  local copies, waits for them, and re-layouts  4.6 us (5%)
  between operations  1.62 us (2%)
    ppermute x25, starting transfers between devices, hop(): lax.ppermute(value, ('src', 'tgt'), [(i, i ^ flip) for i in range(total)])  32.7 us
    ppermute x25, waiting for transfers between devices, hop(): lax.ppermute(value, ('src', 'tgt'), [(i, i ^ flip) for i in range(total)])  27.5 us
    pallas_call x4, Pallas kernels, run(): pl.pallas_call(lambda *refs: pass_kernel(scale, len(parts), first, has_ou...  13.7 us
    pallas_call x1, Pallas kernels, shards(): pl.pallas_call(lambda *refs: product_kernel((src_places, tgt_places), *re...  5.63 us
    pallas_call x1, Pallas kernels, shards(): pl.pallas_call(lambda *refs: list_kernel(src_rows, col_blocks, *refs), ou...  4.07 us
    reduce_sum x8, other arithmetic, half_norms(): return 0.5 * jnp.sum(wide * wide, axis=-1).reshape(-1, TILE)  2.47 us
  transfers between devices with their start and end apart: 25, of which 12 were waited for; matrix products, arithmetic and copies ran while one was open for 8% of the time, Pallas kernels for 14%

profile of v1, /device:TPU:0, one launch (start us, length us, event | category | flops | bytes accessed | tf_op | source)
XLA Modules:
  0.0 95.8 jit_solution(12776955322777586446)
XLA Ops:
  0.6 1.1 %fusion.4 = (bf16[512,256]{1,0:T(8,128)(2,1)S(1)}, bf16[512,256]{1,0:T(8,128)(2,1)S(1)}) fusion(bf16[1024,256]{1,0:T(8,128)(2,1)} %param.8), kind=kLoop, calls=%fused_computation.39 | loop fusion | bytes 1048576 | tf_op jit(solution)/shard_map/slice | solution.py:185
  1.7 3.1 %collective-permute-start.3 = (bf16[4,128,256]{2,1,0:T(8,128)(2,1)S(1)}, bf16[4,128,256]{2,1,0:T(8,128)(2,1)S(1)}, u32[]{:S(2)}, u32[]{:S(2)}) collective-permute-start(bf16[4,128,256]{2,1,0:T(8,128)(2,1)S(1)} %bitcast.42), channel_id=1, source_target_pairs={{0,4},{1,5},{2,6},{3,7},{4,0},{5,1},{6,2},{7,3},{8,12},{9,13},{10,... | collective-permute-start | bytes 786440 | tf_op jit(solution)/shard_map/ppermute | solution.py:22
  4.8 1.5 %collective-permute-start.1 = (bf16[4,128,256]{2,1,0:T(8,128)(2,1)S(1)}, bf16[4,128,256]{2,1,0:T(8,128)(2,1)S(1)}, u32[]{:S(2)}, u32[]{:S(2)}) collective-permute-start(bf16[4,128,256]{2,1,0:T(8,128)(2,1)S(1)} %bitcast.43), channel_id=1, source_target_pairs={{0,2},{1,3},{2,0},{3,1},{4,6},{5,7},{6,4},{7,5},{8,10},{9,11},{10,... | collective-permute-start | bytes 786440 | tf_op jit(solution)/shard_map/ppermute | solution.py:22
  6.3 0.4 collective-permute-start.4
  6.8 0.1 collective-permute-start.2
  7.5 0.7 concatenate.27.refs_1_
  8.2 3.0 %collective-permute-start = (s32[3,128]{1,0:T(4,128)S(1)}, s32[3,128]{1,0:T(4,128)S(1)}, u32[]{:S(2)}, u32[]{:S(2)}) collective-permute-start(s32[3,128]{1,0:T(4,128)S(1)} %concatenate.27.refs_1_), channel_id=1, source_target_pairs={{0,8},{1,9},{2,10},{3,11},{4,12},{5,13},{6,14},{7,15},{8,0},{9,1},... | collective-permute-start | bytes 4616 | tf_op jit(solution)/shard_map/ppermute | solution.py:22
  11.2 1.2 %multiply_reduce_fusion.8 = (f32[512]{0:T(512)S(1)}, f32[512]{0:T(512)S(1)}) fusion(bf16[1024,256]{1,0:T(8,128)(2,1)} %param.8), kind=kLoop, calls=%fused_computation.9 | loop fusion | flops 785408 | bytes 528384 | tf_op jit(solution)/shard_map/reduce_sum | solution.py:27
  12.5 0.7 multiply_bitcast_fusion.1
  13.2 0.8 multiply_bitcast_fusion
  14.0 1.1 %constant_dynamic-slice_fusion.2 = (bf16[4,128,256]{2,1,0:T(8,128)(2,1)S(1)}, bf16[4,128,256]{2,1,0:T(8,128)(2,1)S(1)}) fusion(bf16[16,128,256]{2,1,0:T(8,128)(2,1)} %bitcast.40, s32[]{:T(128)S(6)} %add.39, s32[]{:T(128)S(6)} %select_n.57), kind=kLoop, calls=%fused_computation.30 | loop fusion | bytes 1048584 | tf_op jit(solution)/shard_map/slice | solution.py:190
  15.1 0.1 pad_add_fusion.refs_0_
  15.2 0.9 collective-permute-done.refs_2_
  16.0 3.4 %collective-permute-start.8 = (bf16[4,128,256]{2,1,0:T(8,128)(2,1)S(1)}, bf16[4,128,256]{2,1,0:T(8,128)(2,1)S(1)}, u32[]{:S(2)}, u32[]{:S(2)}) collective-permute-start(bf16[4,128,256]{2,1,0:T(8,128)(2,1)S(1)} %get-tuple-element.18), channel_id=1, source_target_pairs={{0,8},{1,9},{2,10},{3,11},{4,12},{5,13},{6,14},{7,15},{8,0},{9,1},... | collective-permute-start | bytes 786440 | tf_op jit(solution)/shard_map/ppermute | solution.py:22
  19.4 4.1 %tile_lists.1 = (s32[264]{0:T(512)S(1)}, s32[264]{0:T(512)S(1)}, s32[1]{0:T(128)}) custom-call(s32[3]{0:T(128)S(1)} %pad_add_fusion.refs_0_, s32[3,128]{1,0:T(4,128)S(1)} %concatenate.27.refs_1_, s32[3,128]{1,0:T(4,128)S(1)} %collective-permute-done.refs_2_), custom_call_target="tpu_custom_call" | custom-call | tf_op jit(solution)/shard_map/tile_lists/pallas_call | solution.py:199
  23.5 0.0 collective-permute-done.4.refs_14_
  23.5 0.1 collective-permute-start.7
  23.6 0.1 multiply_reduce_fusion.3
  23.7 0.0 collective-permute-done.3.refs_13_
  23.7 3.0 %collective-permute-start.14 = (f32[16,128]{1,0:T(8,128)S(1)}, f32[16,128]{1,0:T(8,128)S(1)}, u32[]{:S(2)}, u32[]{:S(2)}) collective-permute-start(f32[16,128]{1,0:T(8,128)S(1)} %multiply_bitcast_fusion.1), channel_id=1, source_target_pairs={{0,8},{1,9},{2,10},{3,11},{4,12},{5,13},{6,14},{7,15},{8,0},{9,1},... | collective-permute-start | bytes 24584 | tf_op jit(solution)/shard_map/ppermute | solution.py:22
  26.7 0.1 multiply_reduce_fusion.4
  26.9 1.7 %collective-permute-start.5 = (bf16[4,128,256]{2,1,0:T(8,128)(2,1)S(1)}, bf16[4,128,256]{2,1,0:T(8,128)(2,1)S(1)}, u32[]{:S(2)}, u32[]{:S(2)}) collective-permute-start(bf16[4,128,256]{2,1,0:T(8,128)(2,1)S(1)} %collective-permute-done.3.refs_13_), channel_id=1, source_target_pairs={{0,2},{1,3},{2,0},{3,1},{4,6},{5,7},{6,4},{7,5},{8,10},{9,11},{10,... | collective-permute-start | bytes 786440 | tf_op jit(solution)/shard_map/ppermute | solution.py:22
  28.6 0.1 multiply_reduce_fusion.5
  28.8 9.3 %collective-permute-done.8.refs_6_ = bf16[4,128,256]{2,1,0:T(8,128)(2,1)S(1)} collective-permute-done((bf16[4,128,256]{2,1,0:T(8,128)(2,1)S(1)}, bf16[4,128,256]{2,1,0:T(8,128)(2,1)S(1)}, u32[]{:S(2)}, u32[]{:S(2)}) %collective-permute-start.8) | collective-permute-done | bytes 262176 | tf_op jit(solution)/shard_map/ppermute | solution.py:22
  38.0 1.5 %collective-permute-start.6 = (bf16[4,128,256]{2,1,0:T(8,128)(2,1)S(1)}, bf16[4,128,256]{2,1,0:T(8,128)(2,1)S(1)}, u32[]{:S(2)}, u32[]{:S(2)}) collective-permute-start(bf16[4,128,256]{2,1,0:T(8,128)(2,1)S(1)} %collective-permute-done.4.refs_14_), channel_id=1, source_target_pairs={{0,2},{1,3},{2,0},{3,1},{4,6},{5,7},{6,4},{7,5},{8,10},{9,11},{10,... | collective-permute-start | bytes 786440 | tf_op jit(solution)/shard_map/ppermute | solution.py:22
  39.5 2.1 %collective-permute-done.7.refs_5_ = bf16[4,128,256]{2,1,0:T(8,128)(2,1)S(1)} collective-permute-done((bf16[4,128,256]{2,1,0:T(8,128)(2,1)S(1)}, bf16[4,128,256]{2,1,0:T(8,128)(2,1)S(1)}, u32[]{:S(2)}, u32[]{:S(2)}) %collective-permute-start.7) | collective-permute-done | bytes 262176 | tf_op jit(solution)/shard_map/ppermute | solution.py:22
  41.7 0.5 collective-permute-start.9
  42.2 0.1 multiply_reduce_fusion.6
  42.4 2.0 %collective-permute-done.6.refs_16_ = bf16[4,128,256]{2,1,0:T(8,128)(2,1)S(1)} collective-permute-done((bf16[4,128,256]{2,1,0:T(8,128)(2,1)S(1)}, bf16[4,128,256]{2,1,0:T(8,128)(2,1)S(1)}, u32[]{:S(2)}, u32[]{:S(2)}) %collective-permute-start.6) | collective-permute-done | bytes 262176 | tf_op jit(solution)/shard_map/ppermute | solution.py:22
  44.4 0.1 multiply_reduce_fusion.1
  44.6 0.1 multiply_reduce_fusion.2
  44.8 0.6 gather_fusion
  45.3 0.7 multiply_subtract_fusion.refs_3_.refs_4_
  46.1 0.0 copy-start
  46.1 1.2 %copy-done = bf16[2048,256]{1,0:T(8,128)(2,1)S(1)} copy-done((bf16[2048,256]{1,0:T(8,128)(2,1)S(1)}, bf16[2048,256]{1,0:T(8,128)(2,1)}, u32[]{:S(2)}) %copy-start) | copy-done | bytes 1048600
  47.3 5.6 %products.1 = (f32[264,128,128]{2,1,0:T(8,128)S(1)}, f32[264,128,128]{2,1,0:T(8,128)S(1)}) custom-call(s32[3]{0:T(128)S(1)} %pad_add_fusion.refs_0_, s32[264]{0:T(512)S(1)} %get-tuple-element.9.refs_1_.refs_0_, s32[264]{0:T(512)S(1)} %get-tuple-element.10.refs_2_.refs_0_.refs_1_, s32[1]{0:T(128)} %get-tuple-element.11.refs_3_.refs_2_, ...), custom_call_target="tpu_custom_call" | custom-call | tf_op jit(solution)/shard_map/products/pallas_call | solution.py:243
  52.9 3.4 %row_pass.2.refs_3_ = f32[32,128]{1,0:T(8,128)S(1)} custom-call(s32[264]{0:T(512)S(1)} %get-tuple-element.10.refs_2_.refs_0_.refs_1_, s32[264]{0:T(512)S(1)} %get-tuple-element.9.refs_1_.refs_0_, s32[1]{0:T(128)} %get-tuple-element.11.refs_3_.refs_2_, f32[32,128]{1,0:T(8,128)S(1)} %multiply_subtract_fusion.refs_3_.refs_4_, ...), custom_call_target="tpu_custom_call" | custom-call | tf_op jit(solution)/shard_map/row_pass/pallas_call | solution.py:264
  56.3 0.1 collective-permute-start.11
  56.4 0.1 collective-permute-start.12
  56.5 2.7 %collective-permute-start.13 = (f32[32,128]{1,0:T(8,128)S(1)}, f32[32,128]{1,0:T(8,128)S(1)}, u32[]{:S(2)}, u32[]{:S(2)}) collective-permute-start(f32[32,128]{1,0:T(8,128)S(1)} %row_pass.2.refs_3_), channel_id=1, source_target_pairs={{0,9},{1,8},{2,11},{3,10},{4,13},{5,12},{6,15},{7,14},{8,1},{9,0},... | collective-permute-start | bytes 49160 | tf_op jit(solution)/shard_map/ppermute | solution.py:22
  59.2 1.9 %collective-permute-done.12.refs_5_ = f32[32,128]{1,0:T(8,128)S(1)} collective-permute-done((f32[32,128]{1,0:T(8,128)S(1)}, f32[32,128]{1,0:T(8,128)S(1)}, u32[]{:S(2)}, u32[]{:S(2)}) %collective-permute-start.12) | collective-permute-done | bytes 16416 | tf_op jit(solution)/shard_map/ppermute | solution.py:22
  61.1 3.4 %column_pass.2.refs_3_ = f32[32,128]{1,0:T(8,128)S(1)} custom-call(s32[264]{0:T(512)S(1)} %get-tuple-element.9.refs_1_.refs_0_, s32[264]{0:T(512)S(1)} %get-tuple-element.10.refs_2_.refs_0_.refs_1_, s32[1]{0:T(128)} %get-tuple-element.11.refs_3_.refs_2_, f32[32,128]{1,0:T(8,128)S(1)} %row_pass.2.refs_3_, f32[32,128]{1,0:T(8,128)S(1)} %collective-permute-done.11.refs_4_, ...), custom_call_target="tpu_custom_call" | custom-call | tf_op jit(solution)/shard_map/column_pass/pallas_call | solution.py:264
  64.5 1.6 %collective-permute-start.15 = (f32[32,128]{1,0:T(8,128)S(1)}, f32[32,128]{1,0:T(8,128)S(1)}, u32[]{:S(2)}, u32[]{:S(2)}) collective-permute-start(f32[32,128]{1,0:T(8,128)S(1)} %column_pass.2.refs_3_), channel_id=1, source_target_pairs={{0,2},{1,3},{2,0},{3,1},{4,6},{5,7},{6,4},{7,5},{8,10},{9,11},{10,... | collective-permute-start | bytes 49160 | tf_op jit(solution)/shard_map/ppermute | solution.py:22
  66.1 1.8 %collective-permute-start.16 = (f32[32,128]{1,0:T(8,128)S(1)}, f32[32,128]{1,0:T(8,128)S(1)}, u32[]{:S(2)}, u32[]{:S(2)}) collective-permute-start(f32[32,128]{1,0:T(8,128)S(1)} %column_pass.2.refs_3_), channel_id=1, source_target_pairs={{0,4},{1,5},{2,6},{3,7},{4,0},{5,1},{6,2},{7,3},{8,12},{9,13},{10,... | collective-permute-start | bytes 49160 | tf_op jit(solution)/shard_map/ppermute | solution.py:22
  67.9 0.2 collective-permute-start.17
  68.1 0.2 collective-permute-done.15.refs_4_
  68.3 1.5 %collective-permute-done.16.refs_5_ = f32[32,128]{1,0:T(8,128)S(1)} collective-permute-done((f32[32,128]{1,0:T(8,128)S(1)}, f32[32,128]{1,0:T(8,128)S(1)}, u32[]{:S(2)}, u32[]{:S(2)}) %collective-permute-start.16) | collective-permute-done | bytes 16416 | tf_op jit(solution)/shard_map/ppermute | solution.py:22
  69.9 2.7 %collective-permute-done.17.refs_6_ = f32[32,128]{1,0:T(8,128)S(1)} collective-permute-done((f32[32,128]{1,0:T(8,128)S(1)}, f32[32,128]{1,0:T(8,128)S(1)}, u32[]{:S(2)}, u32[]{:S(2)}) %collective-permute-start.17) | collective-permute-done | bytes 16416 | tf_op jit(solution)/shard_map/ppermute | solution.py:22
  72.5 3.4 %row_pass.3.refs_3_ = f32[32,128]{1,0:T(8,128)S(1)} custom-call(s32[264]{0:T(512)S(1)} %get-tuple-element.10.refs_2_.refs_0_.refs_1_, s32[264]{0:T(512)S(1)} %get-tuple-element.9.refs_1_.refs_0_, s32[1]{0:T(128)} %get-tuple-element.11.refs_3_.refs_2_, f32[32,128]{1,0:T(8,128)S(1)} %column_pass.2.refs_3_, f32[32,128]{1,0:T(8,128)S(1)} %collective-permute-done.15.refs_4_, ...), custom_call_target="tpu_custom_call" | custom-call | tf_op jit(solution)/shard_map/row_pass/pallas_call | solution.py:264
  76.0 0.1 collective-permute-start.18
  76.1 0.5 collective-permute-start.19
  76.6 2.2 %collective-permute-start.20 = (f32[32,128]{1,0:T(8,128)S(1)}, f32[32,128]{1,0:T(8,128)S(1)}, u32[]{:S(2)}, u32[]{:S(2)}) collective-permute-start(f32[32,128]{1,0:T(8,128)S(1)} %row_pass.3.refs_3_), channel_id=1, source_target_pairs={{0,9},{1,8},{2,11},{3,10},{4,13},{5,12},{6,15},{7,14},{8,1},{9,0},... | collective-permute-start | bytes 49160 | tf_op jit(solution)/shard_map/ppermute | solution.py:22
  78.8 2.0 %collective-permute-done.19.refs_5_ = f32[32,128]{1,0:T(8,128)S(1)} collective-permute-done((f32[32,128]{1,0:T(8,128)S(1)}, f32[32,128]{1,0:T(8,128)S(1)}, u32[]{:S(2)}, u32[]{:S(2)}) %collective-permute-start.19) | collective-permute-done | bytes 16416 | tf_op jit(solution)/shard_map/ppermute | solution.py:22
  80.8 3.4 %column_pass.3 = (f32[32,128]{1,0:T(8,128)S(1)}, f32[32,128]{1,0:T(8,128)S(1)}) custom-call(s32[264]{0:T(512)S(1)} %get-tuple-element.9.refs_1_.refs_0_, s32[264]{0:T(512)S(1)} %get-tuple-element.10.refs_2_.refs_0_.refs_1_, s32[1]{0:T(128)} %get-tuple-element.11.refs_3_.refs_2_, f32[32,128]{1,0:T(8,128)S(1)} %row_pass.3.refs_3_, ...), custom_call_target="tpu_custom_call" | custom-call | tf_op jit(solution)/shard_map/column_pass/pallas_call | solution.py:264
  84.2 0.7 collective-permute-start.21
  84.9 0.9 collective-permute-start.22
  85.8 2.0 %collective-permute-start.23 = (f32[32,128]{1,0:T(8,128)S(1)}, f32[32,128]{1,0:T(8,128)S(1)}, u32[]{:S(2)}, u32[]{:S(2)}) collective-permute-start(f32[32,128]{1,0:T(8,128)S(1)} %get-tuple-element.15.refs_0_), channel_id=1, source_target_pairs={{0,6},{1,7},{2,4},{3,5},{4,2},{5,3},{6,0},{7,1},{8,14},{9,15},{10,... | collective-permute-start | bytes 49160 | tf_op jit(solution)/shard_map/ppermute | solution.py:22
  87.8 0.3 multiply_reduce_fusion
  88.2 0.5 collective-permute-done.22.refs_2_
  88.7 1.8 %collective-permute-done.23.refs_3_ = f32[32,128]{1,0:T(8,128)S(1)} collective-permute-done((f32[32,128]{1,0:T(8,128)S(1)}, f32[32,128]{1,0:T(8,128)S(1)}, u32[]{:S(2)}, u32[]{:S(2)}) %collective-permute-start.23) | collective-permute-done | bytes 16416 | tf_op jit(solution)/shard_map/ppermute | solution.py:22
  90.5 1.6 %collective-permute-start.24 = (f32[32,128]{1,0:T(8,128)S(1)}, f32[32,128]{1,0:T(8,128)S(1)}, u32[]{:S(2)}, u32[]{:S(2)}) collective-permute-start(f32[32,128]{1,0:T(8,128)S(1)} %finish.1), channel_id=1, source_target_pairs={{0,8},{1,9},{2,10},{3,11},{4,12},{5,13},{6,14},{7,15},{8,0},{9,1},... | collective-permute-start | bytes 49160 | tf_op jit(solution)/shard_map/ppermute | solution.py:22
  92.1 0.6 fusion.2
  92.7 2.5 %collective-permute-done.24 = f32[32,128]{1,0:T(8,128)S(1)} collective-permute-done((f32[32,128]{1,0:T(8,128)S(1)}, f32[32,128]{1,0:T(8,128)S(1)}, u32[]{:S(2)}, u32[]{:S(2)}) %collective-permute-start.24) | collective-permute-done | bytes 16416 | tf_op jit(solution)/shard_map/ppermute | solution.py:22
  95.2 0.6 fusion
  (30 shorter events, 0.1 us)
Async XLA Ops:
  1.7 22.0 %collective-permute-start.3 = (bf16[4,128,256]{2,1,0:T(8,128)(2,1)S(1)}, bf16[4,128,256]{2,1,0:T(8,128)(2,1)S(1)}, u32[]{:S(2)}, u32[]{:S(2)}) collective-permute-start(bf16[4,128,256]{2,1,0:T(8,128)(2,1)S(1)} %bitcast.42), channel_id=1, source_target_pairs={{0,4},{1,5},{2,6},{3,7},{4,0},{5,1},{6,2},{7,3},{8,12},{9,13},{10,... | collective-permute-start | bytes 786440 | tf_op jit(solution)/shard_map/ppermute | solution.py:22
  4.8 36.9 %collective-permute-start.1 = (bf16[4,128,256]{2,1,0:T(8,128)(2,1)S(1)}, bf16[4,128,256]{2,1,0:T(8,128)(2,1)S(1)}, u32[]{:S(2)}, u32[]{:S(2)}) collective-permute-start(bf16[4,128,256]{2,1,0:T(8,128)(2,1)S(1)} %bitcast.43), channel_id=1, source_target_pairs={{0,2},{1,3},{2,0},{3,1},{4,6},{5,7},{6,4},{7,5},{8,10},{9,11},{10,... | collective-permute-start | bytes 786440 | tf_op jit(solution)/shard_map/ppermute | solution.py:22
  6.3 17.2 %collective-permute-start.4 = (bf16[4,128,256]{2,1,0:T(8,128)(2,1)S(1)}, bf16[4,128,256]{2,1,0:T(8,128)(2,1)S(1)}, u32[]{:S(2)}, u32[]{:S(2)}) collective-permute-start(bf16[4,128,256]{2,1,0:T(8,128)(2,1)S(1)} %bitcast.45), channel_id=1, source_target_pairs={{0,4},{1,5},{2,6},{3,7},{4,0},{5,1},{6,2},{7,3},{8,12},{9,13},{10,... | collective-permute-start | bytes 786440 | tf_op jit(solution)/shard_map/ppermute | solution.py:22
  6.8 20.1 %collective-permute-start.2 = (bf16[4,128,256]{2,1,0:T(8,128)(2,1)S(1)}, bf16[4,128,256]{2,1,0:T(8,128)(2,1)S(1)}, u32[]{:S(2)}, u32[]{:S(2)}) collective-permute-start(bf16[4,128,256]{2,1,0:T(8,128)(2,1)S(1)} %bitcast.46), channel_id=1, source_target_pairs={{0,2},{1,3},{2,0},{3,1},{4,6},{5,7},{6,4},{7,5},{8,10},{9,11},{10,... | collective-permute-start | bytes 786440 | tf_op jit(solution)/shard_map/ppermute | solution.py:22
  8.2 7.8 %collective-permute-start = (s32[3,128]{1,0:T(4,128)S(1)}, s32[3,128]{1,0:T(4,128)S(1)}, u32[]{:S(2)}, u32[]{:S(2)}) collective-permute-start(s32[3,128]{1,0:T(4,128)S(1)} %concatenate.27.refs_1_), channel_id=1, source_target_pairs={{0,8},{1,9},{2,10},{3,11},{4,12},{5,13},{6,14},{7,15},{8,0},{9,1},... | collective-permute-start | bytes 4616 | tf_op jit(solution)/shard_map/ppermute | solution.py:22
  16.0 22.0 %collective-permute-start.8 = (bf16[4,128,256]{2,1,0:T(8,128)(2,1)S(1)}, bf16[4,128,256]{2,1,0:T(8,128)(2,1)S(1)}, u32[]{:S(2)}, u32[]{:S(2)}) collective-permute-start(bf16[4,128,256]{2,1,0:T(8,128)(2,1)S(1)} %get-tuple-element.18), channel_id=1, source_target_pairs={{0,8},{1,9},{2,10},{3,11},{4,12},{5,13},{6,14},{7,15},{8,0},{9,1},... | collective-permute-start | bytes 786440 | tf_op jit(solution)/shard_map/ppermute | solution.py:22
  23.5 18.2 %collective-permute-start.7 = (bf16[4,128,256]{2,1,0:T(8,128)(2,1)S(1)}, bf16[4,128,256]{2,1,0:T(8,128)(2,1)S(1)}, u32[]{:S(2)}, u32[]{:S(2)}) collective-permute-start(bf16[4,128,256]{2,1,0:T(8,128)(2,1)S(1)} %get-tuple-element.19), channel_id=1, source_target_pairs={{0,8},{1,9},{2,10},{3,11},{4,12},{5,13},{6,14},{7,15},{8,0},{9,1},... | collective-permute-start | bytes 786440 | tf_op jit(solution)/shard_map/ppermute | solution.py:22
  23.7 35.4 %collective-permute-start.14 = (f32[16,128]{1,0:T(8,128)S(1)}, f32[16,128]{1,0:T(8,128)S(1)}, u32[]{:S(2)}, u32[]{:S(2)}) collective-permute-start(f32[16,128]{1,0:T(8,128)S(1)} %multiply_bitcast_fusion.1), channel_id=1, source_target_pairs={{0,8},{1,9},{2,10},{3,11},{4,12},{5,13},{6,14},{7,15},{8,0},{9,1},... | collective-permute-start | bytes 24584 | tf_op jit(solution)/shard_map/ppermute | solution.py:22
  26.9 17.7 %collective-permute-start.5 = (bf16[4,128,256]{2,1,0:T(8,128)(2,1)S(1)}, bf16[4,128,256]{2,1,0:T(8,128)(2,1)S(1)}, u32[]{:S(2)}, u32[]{:S(2)}) collective-permute-start(bf16[4,128,256]{2,1,0:T(8,128)(2,1)S(1)} %collective-permute-done.3.refs_13_), channel_id=1, source_target_pairs={{0,2},{1,3},{2,0},{3,1},{4,6},{5,7},{6,4},{7,5},{8,10},{9,11},{10,... | collective-permute-start | bytes 786440 | tf_op jit(solution)/shard_map/ppermute | solution.py:22
  38.0 6.4 %collective-permute-start.6 = (bf16[4,128,256]{2,1,0:T(8,128)(2,1)S(1)}, bf16[4,128,256]{2,1,0:T(8,128)(2,1)S(1)}, u32[]{:S(2)}, u32[]{:S(2)}) collective-permute-start(bf16[4,128,256]{2,1,0:T(8,128)(2,1)S(1)} %collective-permute-done.4.refs_14_), channel_id=1, source_target_pairs={{0,2},{1,3},{2,0},{3,1},{4,6},{5,7},{6,4},{7,5},{8,10},{9,11},{10,... | collective-permute-start | bytes 786440 | tf_op jit(solution)/shard_map/ppermute | solution.py:22
  41.7 4.4 %collective-permute-start.10 = (bf16[4,128,256]{2,1,0:T(8,128)(2,1)S(1)}, bf16[4,128,256]{2,1,0:T(8,128)(2,1)S(1)}, u32[]{:S(2)}, u32[]{:S(2)}) collective-permute-start(bf16[4,128,256]{2,1,0:T(8,128)(2,1)S(1)} %collective-permute-done.8.refs_6_), channel_id=1, source_target_pairs={{0,1},{1,0},{2,3},{3,2},{4,5},{5,4},{6,7},{7,6},{8,9},{9,8},{10,11... | collective-permute-start | bytes 786440 | tf_op jit(solution)/shard_map/ppermute | solution.py:22
  41.7 4.4 %collective-permute-start.9 = (bf16[4,128,256]{2,1,0:T(8,128)(2,1)S(1)}, bf16[4,128,256]{2,1,0:T(8,128)(2,1)S(1)}, u32[]{:S(2)}, u32[]{:S(2)}) collective-permute-start(bf16[4,128,256]{2,1,0:T(8,128)(2,1)S(1)} %collective-permute-done.7.refs_5_), channel_id=1, source_target_pairs={{0,1},{1,0},{2,3},{3,2},{4,5},{5,4},{6,7},{7,6},{8,9},{9,8},{10,11... | collective-permute-start | bytes 786440 | tf_op jit(solution)/shard_map/ppermute | solution.py:22
  46.1 1.2 %copy-start = (bf16[2048,256]{1,0:T(8,128)(2,1)S(1)}, bf16[2048,256]{1,0:T(8,128)(2,1)}, u32[]{:S(2)}) copy-start(bf16[2048,256]{1,0:T(8,128)(2,1)} %param.7) | copy-start | bytes 3145732
  56.3 2.9 %collective-permute-start.11 = (f32[32,128]{1,0:T(8,128)S(1)}, f32[32,128]{1,0:T(8,128)S(1)}, u32[]{:S(2)}, u32[]{:S(2)}) collective-permute-start(f32[32,128]{1,0:T(8,128)S(1)} %row_pass.2.refs_3_), channel_id=1, source_target_pairs={{0,1},{1,0},{2,3},{3,2},{4,5},{5,4},{6,7},{7,6},{8,9},{9,8},{10,11... | collective-permute-start | bytes 49160 | tf_op jit(solution)/shard_map/ppermute | solution.py:22
  56.4 4.7 %collective-permute-start.12 = (f32[32,128]{1,0:T(8,128)S(1)}, f32[32,128]{1,0:T(8,128)S(1)}, u32[]{:S(2)}, u32[]{:S(2)}) collective-permute-start(f32[32,128]{1,0:T(8,128)S(1)} %row_pass.2.refs_3_), channel_id=1, source_target_pairs={{0,8},{1,9},{2,10},{3,11},{4,12},{5,13},{6,14},{7,15},{8,0},{9,1},... | collective-permute-start | bytes 49160 | tf_op jit(solution)/shard_map/ppermute | solution.py:22
  56.5 4.6 %collective-permute-start.13 = (f32[32,128]{1,0:T(8,128)S(1)}, f32[32,128]{1,0:T(8,128)S(1)}, u32[]{:S(2)}, u32[]{:S(2)}) collective-permute-start(f32[32,128]{1,0:T(8,128)S(1)} %row_pass.2.refs_3_), channel_id=1, source_target_pairs={{0,9},{1,8},{2,11},{3,10},{4,13},{5,12},{6,15},{7,14},{8,1},{9,0},... | collective-permute-start | bytes 49160 | tf_op jit(solution)/shard_map/ppermute | solution.py:22
  64.5 3.8 %collective-permute-start.15 = (f32[32,128]{1,0:T(8,128)S(1)}, f32[32,128]{1,0:T(8,128)S(1)}, u32[]{:S(2)}, u32[]{:S(2)}) collective-permute-start(f32[32,128]{1,0:T(8,128)S(1)} %column_pass.2.refs_3_), channel_id=1, source_target_pairs={{0,2},{1,3},{2,0},{3,1},{4,6},{5,7},{6,4},{7,5},{8,10},{9,11},{10,... | collective-permute-start | bytes 49160 | tf_op jit(solution)/shard_map/ppermute | solution.py:22
  66.1 3.7 %collective-permute-start.16 = (f32[32,128]{1,0:T(8,128)S(1)}, f32[32,128]{1,0:T(8,128)S(1)}, u32[]{:S(2)}, u32[]{:S(2)}) collective-permute-start(f32[32,128]{1,0:T(8,128)S(1)} %column_pass.2.refs_3_), channel_id=1, source_target_pairs={{0,4},{1,5},{2,6},{3,7},{4,0},{5,1},{6,2},{7,3},{8,12},{9,13},{10,... | collective-permute-start | bytes 49160 | tf_op jit(solution)/shard_map/ppermute | solution.py:22
  67.9 4.6 %collective-permute-start.17 = (f32[32,128]{1,0:T(8,128)S(1)}, f32[32,128]{1,0:T(8,128)S(1)}, u32[]{:S(2)}, u32[]{:S(2)}) collective-permute-start(f32[32,128]{1,0:T(8,128)S(1)} %column_pass.2.refs_3_), channel_id=1, source_target_pairs={{0,6},{1,7},{2,4},{3,5},{4,2},{5,3},{6,0},{7,1},{8,14},{9,15},{10,... | collective-permute-start | bytes 49160 | tf_op jit(solution)/shard_map/ppermute | solution.py:22
  68.1 19.7 %copy-start.1 = (bf16[2048,256]{1,0:T(8,128)(2,1)S(1)}, bf16[2048,256]{1,0:T(8,128)(2,1)}, u32[]{:S(2)}) copy-start(bf16[2048,256]{1,0:T(8,128)(2,1)} %param.7) | copy-start | bytes 3145732
  76.0 2.8 %collective-permute-start.18 = (f32[32,128]{1,0:T(8,128)S(1)}, f32[32,128]{1,0:T(8,128)S(1)}, u32[]{:S(2)}, u32[]{:S(2)}) collective-permute-start(f32[32,128]{1,0:T(8,128)S(1)} %row_pass.3.refs_3_), channel_id=1, source_target_pairs={{0,1},{1,0},{2,3},{3,2},{4,5},{5,4},{6,7},{7,6},{8,9},{9,8},{10,11... | collective-permute-start | bytes 49160 | tf_op jit(solution)/shard_map/ppermute | solution.py:22
  76.1 4.8 %collective-permute-start.19 = (f32[32,128]{1,0:T(8,128)S(1)}, f32[32,128]{1,0:T(8,128)S(1)}, u32[]{:S(2)}, u32[]{:S(2)}) collective-permute-start(f32[32,128]{1,0:T(8,128)S(1)} %row_pass.3.refs_3_), channel_id=1, source_target_pairs={{0,8},{1,9},{2,10},{3,11},{4,12},{5,13},{6,14},{7,15},{8,0},{9,1},... | collective-permute-start | bytes 49160 | tf_op jit(solution)/shard_map/ppermute | solution.py:22
  76.6 4.2 %collective-permute-start.20 = (f32[32,128]{1,0:T(8,128)S(1)}, f32[32,128]{1,0:T(8,128)S(1)}, u32[]{:S(2)}, u32[]{:S(2)}) collective-permute-start(f32[32,128]{1,0:T(8,128)S(1)} %row_pass.3.refs_3_), channel_id=1, source_target_pairs={{0,9},{1,8},{2,11},{3,10},{4,13},{5,12},{6,15},{7,14},{8,1},{9,0},... | collective-permute-start | bytes 49160 | tf_op jit(solution)/shard_map/ppermute | solution.py:22
  84.2 3.9 %collective-permute-start.21 = (f32[32,128]{1,0:T(8,128)S(1)}, f32[32,128]{1,0:T(8,128)S(1)}, u32[]{:S(2)}, u32[]{:S(2)}) collective-permute-start(f32[32,128]{1,0:T(8,128)S(1)} %get-tuple-element.15.refs_0_), channel_id=1, source_target_pairs={{0,2},{1,3},{2,0},{3,1},{4,6},{5,7},{6,4},{7,5},{8,10},{9,11},{10,... | collective-permute-start | bytes 49160 | tf_op jit(solution)/shard_map/ppermute | solution.py:22
  84.9 3.7 %collective-permute-start.22 = (f32[32,128]{1,0:T(8,128)S(1)}, f32[32,128]{1,0:T(8,128)S(1)}, u32[]{:S(2)}, u32[]{:S(2)}) collective-permute-start(f32[32,128]{1,0:T(8,128)S(1)} %get-tuple-element.15.refs_0_), channel_id=1, source_target_pairs={{0,4},{1,5},{2,6},{3,7},{4,0},{5,1},{6,2},{7,3},{8,12},{9,13},{10,... | collective-permute-start | bytes 49160 | tf_op jit(solution)/shard_map/ppermute | solution.py:22
  85.8 4.6 %collective-permute-start.23 = (f32[32,128]{1,0:T(8,128)S(1)}, f32[32,128]{1,0:T(8,128)S(1)}, u32[]{:S(2)}, u32[]{:S(2)}) collective-permute-start(f32[32,128]{1,0:T(8,128)S(1)} %get-tuple-element.15.refs_0_), channel_id=1, source_target_pairs={{0,6},{1,7},{2,4},{3,5},{4,2},{5,3},{6,0},{7,1},{8,14},{9,15},{10,... | collective-permute-start | bytes 49160 | tf_op jit(solution)/shard_map/ppermute | solution.py:22
  90.5 4.7 %collective-permute-start.24 = (f32[32,128]{1,0:T(8,128)S(1)}, f32[32,128]{1,0:T(8,128)S(1)}, u32[]{:S(2)}, u32[]{:S(2)}) collective-permute-start(f32[32,128]{1,0:T(8,128)S(1)} %finish.1), channel_id=1, source_target_pairs={{0,8},{1,9},{2,10},{3,11},{4,12},{5,13},{6,14},{7,15},{8,0},{9,1},... | collective-permute-start | bytes 49160 | tf_op jit(solution)/shard_map/ppermute | solution.py:22
